TPU v7x, 256 devices: a whole 4x4x8 slice. The times are simulated.
256 devices in a mesh: segment: 8 (over z_lo, y), dp: 32 (over z_hi, x, core).
Axes of the slice: x: 4, y: 4, z: 8 (z_hi: 4, z_lo: 2; z = z_hi * 2 + z_lo), core: 2. Of those that a mesh axis runs over, the one named last changes fastest.
Arguments:
- handoff: float32 [8, 128, 8, 8, 512], P('segment', 'dp'), parts along dimension 1, may hold values from -6 to 6
- fresh: float32 [4, 128, 8, 8, 512], P(None, 'dp'), parts along dimension 1, may hold values from -6 to 6
- skip_queue: float32 [8, 7, 128, 8, 8, 512], P('segment', None, 'dp'), parts along dimension 2, may hold values from -6 to 6
- conv_weight: bfloat16 [8, 2, 4608, 512], P('segment'), may hold values from -0.09375 to 0.09375
- norm_gain: float32 [8, 2, 512], P('segment'), may hold values from 0.5 to 1.5
- norm_shift: float32 [8, 2, 512], P('segment'), may hold values from -3 to 3
Outputs:
- activations: float32 [8, 5, 128, 8, 8, 512], P('segment', None, 'dp'), parts along dimension 2
- queue_out: float32 [8, 7, 128, 8, 8, 512], P('segment', None, 'dp'), parts along dimension 2
There are 32 independent parts, one for each index of `dp`. A program takes and returns all parts, laid end to end along the dimension named above; an argument that names none is the same for every part. Nothing has to cross between parts.
All inputs are finite; a program needn't handle non-finite values.
Results may differ from a plain program's by a relative error of at most 0.004.
Values sent between devices are 32-bit elements; how exact they have to be, the bound alone decides.
A program may use at most 128 MiB of HBM per device.

v0:
```python
import jax
import jax.numpy as jnp
from jax import lax
from jax.sharding import PartitionSpec as P

GROUP = 16


norm_eps = 1e-05


def from_partner(value, axis, distance):
    mask = 2**distance
    pairs = [(source, source ^ mask) for source in range(lax.axis_size(axis))]
    return lax.ppermute(value, axis, pairs)


def from_behind(array, axis, by):
    devices = lax.axis_size(axis)
    pairs = [(i, i + by) for i in range(devices) if 0 <= i + by < devices]
    return lax.ppermute(array, axis, pairs)


def group_silu(field, gain_row, shift_row):
    images, height_cells, width_cells, channels = field.shape
    grouped = field.reshape(images, height_cells * width_cells, channels // GROUP, GROUP)
    average = jnp.mean(grouped, axis=(1, 3), keepdims=True)
    spread = jnp.mean(jnp.square(grouped - average), axis=(1, 3), keepdims=True)
    normed = ((grouped - average) * lax.rsqrt(spread + norm_eps)).reshape(field.shape)
    scaled = normed * gain_row + shift_row
    return jax.nn.silu(scaled).astype(jnp.bfloat16)


def convolve(activated, kernel):
    images, height_cells, width_cells, channels = activated.shape
    padded = jnp.pad(activated, ((0, 0), (1, 1), (1, 1), (0, 0)))
    patches = jnp.concatenate(
        [
            padded[:, row_off : row_off + height_cells, col_off : col_off + width_cells, :]
            for row_off in range(3)
            for col_off in range(3)
        ],
        axis=3,
    )
    product = jnp.dot(
        patches.reshape(images * height_cells * width_cells, 9 * channels),
        kernel,
        preferred_element_type=jnp.float32,
    )
    return product.reshape(images, height_cells, width_cells, kernel.shape[1])


def section(entering, skip_map, kernels, gain_rows, shift_rows, is_encoder):
    first_conv = convolve(group_silu(entering, gain_rows[0], shift_rows[0]), kernels[0])
    feed_map = jnp.where(is_encoder, first_conv, skip_map)
    second = convolve(group_silu(feed_map, gain_rows[1], shift_rows[1]), kernels[1])
    return entering + second + jnp.where(is_encoder, jnp.float32(0.0), first_conv)


def per_device(handoff, fresh, skip_queue, conv_weight, norm_gain, norm_shift):
    segments_all = lax.axis_size("segment")
    my_index = lax.axis_index("segment")
    is_encoder = my_index < segments_all // 2
    queue_depth = 2 * my_index - segments_all + 1
    slot_ids = jnp.arange(skip_queue.shape[1])
    insert = (slot_ids == queue_depth - 1) & jnp.logical_not(is_encoder)
    filled = (slot_ids < queue_depth) & jnp.logical_not(is_encoder)
    ticks_all = fresh.shape[0] + 1
    inputs_now = handoff[0]
    pending = skip_queue[0]
    kernels = conv_weight[0]
    gain_rows = norm_gain[0]
    shift_rows = norm_shift[0]
    history = []
    for tick_index in range(ticks_all):
        result = section(inputs_now, pending[0], kernels, gain_rows, shift_rows, is_encoder)
        history.append(result)
        received = result
        for bit_index in range(segments_all.bit_length() - 1):
            received = from_partner(received, "segment", bit_index)
        shifted = jnp.concatenate([pending[1:], jnp.zeros_like(pending[:1])], axis=0)
        pending = jnp.where(insert[:, None, None, None, None], received[None], shifted)
        if tick_index + 1 < ticks_all:
            passed = from_behind(result, "segment", 1)
            inputs_now = jnp.where(my_index == 0, fresh[tick_index], passed)
    activations = jnp.stack(history, axis=0)[None]
    queue_out = jnp.where(filled[:, None, None, None, None], pending, jnp.float32(0.0))[None]
    return (activations, queue_out)


def solution(mesh):
    return jax.shard_map(
        per_device,
        mesh=mesh,
        in_specs=(
            P("segment", "dp", None, None, None),
            P(None, "dp", None, None, None),
            P("segment", None, "dp", None, None, None),
            P("segment", None, None, None),
            P("segment", None, None),
            P("segment", None, None),
        ),
        out_specs=(
            P("segment", None, "dp", None, None, None),
            P("segment", None, "dp", None, None, None),
        ),
        check_vma=False,
    )
```

profile of v0, /device:TPU:174, one launch (start us, length us, event | category | flops | bytes accessed | tf_op | source)
XLA Modules:
  0.0 292.6 jit_solution(5549832101218233723)
XLA Ops:
  0.6 0.8 fusion.160
  1.4 0.8 fusion.161
  2.2 1.1 reduce_sum.233
  3.7 1.1 multiply_reduce_fusion.9
  5.2 1.2 multiply_convert_fusion.9
  6.6 0.2 constant_dynamic-update-slice_fusion
  7.1 1.4 copy-done.8
  8.5 4.5 %fusion.159 = (f32[4,512]{1,0:T(4,128)S(1)}, f32[4,8,8,512]{3,2,1,0:T(8,128)S(1)}, f32[4,8,8,512]{3,2,1,0:T(8,128)S(1)}) fusion(f32[1,7,4,8,8,512]{5,4,3,2,1,0:T(8,128)} %param.8, pred[]{:T(512)S(6)} %lt.13, bf16[4,8,8,4608]{3,2,1,0:T(8,128)(2,1)} %copy-done.8, bf16[1,2,4608,512]{3,2,1,0:T(8,128)(2,1)} %param.9), kind=kOutput, calls=%fused_computation.288 | convolution fusion | flops 1208219648 | bytes 8658945 | tf_op jit(solution)/shard_map/dot_general | solution.py:45
  13.8 0.2 multiply_convert_fusion.8
  14.7 4.7 %bitcast_dynamic-update-slice_fusion.4 = (f32[5,4,8,8,512]{4,3,2,1,0:T(8,128)}, f32[4,8,8,512]{3,2,1,0:T(8,128)}) fusion(f32[4,8,8,512]{3,2,1,0:T(8,128)S(1)} %get-tuple-element.24, pred[]{:T(512)S(6)} %lt.13, bf16[4,8,8,4608]{3,2,1,0:T(8,128)(2,1)S(1)} %fusion.82, bf16[1,2,4608,512]{3,2,1,0:T(8,128)(2,1)} %param.9, f32[1,4,8,8,512]{4,3,2,1,0:T(8,128)S(1)} %copy-done.4), kind=kOutput, calls=%fused_computation.142 | convolution fusion | flops 1208352768 | bytes 9175041 | tf_op jit(solution)/shard_map/dot_general | solution.py:45
  19.4 3.5 %collective-permute-start = (f32[4,8,8,512]{3,2,1,0:T(8,128)}, f32[4,8,8,512]{3,2,1,0:T(8,128)}, u32[]{:S(2)}, u32[]{:S(2)}) collective-permute-start(f32[4,8,8,512]{3,2,1,0:T(8,128)} %get-tuple-element.26), channel_id=1, source_target_pairs={{0,32},{32,64},{64,96},{96,128},{128,160},{160,192},{192,224},{1,3... | collective-permute-start | bytes 1572872 | tf_op jit(solution)/shard_map/ppermute | solution.py:21
  22.8 0.5 collective-permute-start.1
  23.4 2.3 slice_bitcast_fusion
  25.7 10.7 %collective-permute-done = f32[4,8,8,512]{3,2,1,0:T(8,128)} collective-permute-done((f32[4,8,8,512]{3,2,1,0:T(8,128)}, f32[4,8,8,512]{3,2,1,0:T(8,128)}, u32[]{:S(2)}, u32[]{:S(2)}) %collective-permute-start) | collective-permute-done | bytes 524320 | tf_op jit(solution)/shard_map/ppermute | solution.py:21
  36.4 2.1 fusion.158
  38.8 1.1 multiply_reduce_fusion.7
  40.4 6.1 %collective-permute-done.1 = f32[4,8,8,512]{3,2,1,0:T(8,128)} collective-permute-done((f32[4,8,8,512]{3,2,1,0:T(8,128)}, f32[4,8,8,512]{3,2,1,0:T(8,128)}, u32[]{:S(2)}, u32[]{:S(2)}) %collective-permute-start.1) | collective-permute-done | bytes 524320 | tf_op jit(solution)/shard_map/ppermute | solution.py:15
  46.5 2.3 collective-permute-start.2
  48.8 1.2 multiply_convert_fusion.7
  50.2 10.8 %collective-permute-done.2 = f32[4,8,8,512]{3,2,1,0:T(8,128)S(1)} collective-permute-done((f32[4,8,8,512]{3,2,1,0:T(8,128)}, f32[4,8,8,512]{3,2,1,0:T(8,128)S(1)}, u32[]{:S(2)}, u32[]{:S(2)}) %collective-permute-start.2) | collective-permute-done | bytes 524320 | tf_op jit(solution)/shard_map/ppermute | solution.py:15
  61.0 1.0 collective-permute-start.3
  62.4 10.5 %collective-permute-done.3 = f32[4,8,8,512]{3,2,1,0:T(8,128)S(1)} collective-permute-done((f32[4,8,8,512]{3,2,1,0:T(8,128)S(1)}, f32[4,8,8,512]{3,2,1,0:T(8,128)S(1)}, u32[]{:S(2)}, u32[]{:S(2)}) %collective-permute-start.3) | collective-permute-done | bytes 524320 | tf_op jit(solution)/shard_map/ppermute | solution.py:15
  72.8 0.6 pad_select_fusion.3
  73.5 5.9 %fusion.156 = (f32[4,512]{1,0:T(4,128)S(1)}, f32[4,8,8,512]{3,2,1,0:T(8,128)S(1)}, f32[4,8,8,512]{3,2,1,0:T(8,128)}) fusion(f32[7,4,8,8,512]{4,3,2,1,0:T(8,128)S(1)} %pad_select_fusion.3, pred[]{:T(512)S(6)} %lt.13, bf16[4,8,8,4608]{3,2,1,0:T(8,128)(2,1)S(1)} %fusion.90, bf16[1,2,4608,512]{3,2,1,0:T(8,128)(2,1)} %param.9), kind=kOutput, calls=%fused_computation.286 | convolution fusion | flops 1208219648 | bytes 8658945 | tf_op jit(solution)/shard_map/dot_general | solution.py:45
  81.1 0.5 copy-done.6
  81.7 4.7 %bitcast_dynamic-update-slice_fusion.3 = (f32[5,4,8,8,512]{4,3,2,1,0:T(8,128)}, f32[4,8,8,512]{3,2,1,0:T(8,128)}) fusion(f32[5,4,8,8,512]{4,3,2,1,0:T(8,128)} %get-tuple-element.25, f32[4,8,8,512]{3,2,1,0:T(8,128)S(1)} %copy-done.9, pred[]{:T(512)S(6)} %lt.13, f32[4,8,8,512]{3,2,1,0:T(8,128)S(1)} %copy-done.6, bf16[4,8,8,4608]{3,2,1,0:T(8,128)(2,1)S(1)} %fusion.98, ...), kind=kOutput, calls=%fused_computation.140 | convolution fusion | flops 1208352768 | bytes 9175041 | tf_op jit(solution)/shard_map/dot_general | solution.py:45
  86.3 2.4 collective-permute-start.4
  88.8 1.9 collective-permute-start.5
  90.7 12.8 %collective-permute-done.4 = f32[4,8,8,512]{3,2,1,0:T(8,128)S(1)} collective-permute-done((f32[4,8,8,512]{3,2,1,0:T(8,128)}, f32[4,8,8,512]{3,2,1,0:T(8,128)S(1)}, u32[]{:S(2)}, u32[]{:S(2)}) %collective-permute-start.4) | collective-permute-done | bytes 524320 | tf_op jit(solution)/shard_map/ppermute | solution.py:21
  104.4 6.8 %collective-permute-done.5 = f32[4,8,8,512]{3,2,1,0:T(8,128)} collective-permute-done((f32[4,8,8,512]{3,2,1,0:T(8,128)}, f32[4,8,8,512]{3,2,1,0:T(8,128)}, u32[]{:S(2)}, u32[]{:S(2)}) %collective-permute-start.5) | collective-permute-done | bytes 524320 | tf_op jit(solution)/shard_map/ppermute | solution.py:15
  111.3 4.6 %collective-permute-start.6 = (f32[4,8,8,512]{3,2,1,0:T(8,128)}, f32[4,8,8,512]{3,2,1,0:T(8,128)S(1)}, u32[]{:S(2)}, u32[]{:S(2)}) collective-permute-start(f32[4,8,8,512]{3,2,1,0:T(8,128)} %collective-permute-done.5), channel_id=1, source_target_pairs={{0,64},{32,96},{64,0},{96,32},{128,192},{160,224},{192,128},{224,1... | collective-permute-start | bytes 1572872 | tf_op jit(solution)/shard_map/ppermute | solution.py:15
  116.3 7.0 %collective-permute-done.6 = f32[4,8,8,512]{3,2,1,0:T(8,128)S(1)} collective-permute-done((f32[4,8,8,512]{3,2,1,0:T(8,128)}, f32[4,8,8,512]{3,2,1,0:T(8,128)S(1)}, u32[]{:S(2)}, u32[]{:S(2)}) %collective-permute-start.6) | collective-permute-done | bytes 524320 | tf_op jit(solution)/shard_map/ppermute | solution.py:15
  123.2 1.0 collective-permute-start.7
  124.6 7.8 %collective-permute-done.7 = f32[4,8,8,512]{3,2,1,0:T(8,128)S(1)} collective-permute-done((f32[4,8,8,512]{3,2,1,0:T(8,128)S(1)}, f32[4,8,8,512]{3,2,1,0:T(8,128)S(1)}, u32[]{:S(2)}, u32[]{:S(2)}) %collective-permute-start.7) | collective-permute-done | bytes 524320 | tf_op jit(solution)/shard_map/ppermute | solution.py:15
  132.4 0.5 pad_select_fusion.2
  132.9 5.8 %fusion.153 = (f32[4,512]{1,0:T(4,128)S(1)}, f32[4,8,8,512]{3,2,1,0:T(8,128)S(1)}, f32[4,8,8,512]{3,2,1,0:T(8,128)}) fusion(f32[7,4,8,8,512]{4,3,2,1,0:T(8,128)S(1)} %pad_select_fusion.2, pred[]{:T(512)S(6)} %lt.13, bf16[4,8,8,4608]{3,2,1,0:T(8,128)(2,1)S(1)} %fusion.106, bf16[1,2,4608,512]{3,2,1,0:T(8,128)(2,1)} %param.9), kind=kOutput, calls=%fused_computation.284 | convolution fusion | flops 1208219648 | bytes 8658945 | tf_op jit(solution)/shard_map/dot_general | solution.py:45
  140.5 0.5 copy-done.10
  140.9 4.7 %bitcast_dynamic-update-slice_fusion.2 = (f32[5,4,8,8,512]{4,3,2,1,0:T(8,128)}, f32[4,8,8,512]{3,2,1,0:T(8,128)}) fusion(f32[5,4,8,8,512]{4,3,2,1,0:T(8,128)} %get-tuple-element.28, f32[4,8,8,512]{3,2,1,0:T(8,128)S(1)} %copy-done.10, pred[]{:T(512)S(6)} %lt.13, f32[4,8,8,512]{3,2,1,0:T(8,128)S(1)} %get-tuple-element.13, ...), kind=kOutput, calls=%fused_computation.138 | convolution fusion | flops 1208352768 | bytes 9175041 | tf_op jit(solution)/shard_map/dot_general | solution.py:45
  145.6 3.5 %collective-permute-start.8 = (f32[4,8,8,512]{3,2,1,0:T(8,128)}, f32[4,8,8,512]{3,2,1,0:T(8,128)S(1)}, u32[]{:S(2)}, u32[]{:S(2)}) collective-permute-start(f32[4,8,8,512]{3,2,1,0:T(8,128)} %get-tuple-element.32), channel_id=1, source_target_pairs={{0,32},{32,64},{64,96},{96,128},{128,160},{160,192},{192,224},{1,3... | collective-permute-start | bytes 1572872 | tf_op jit(solution)/shard_map/ppermute | solution.py:21
  149.1 0.8 collective-permute-start.9
  149.9 12.8 %collective-permute-done.8 = f32[4,8,8,512]{3,2,1,0:T(8,128)S(1)} collective-permute-done((f32[4,8,8,512]{3,2,1,0:T(8,128)}, f32[4,8,8,512]{3,2,1,0:T(8,128)S(1)}, u32[]{:S(2)}, u32[]{:S(2)}) %collective-permute-start.8) | collective-permute-done | bytes 524320 | tf_op jit(solution)/shard_map/ppermute | solution.py:21
  163.8 9.6 %collective-permute-done.9 = f32[4,8,8,512]{3,2,1,0:T(8,128)} collective-permute-done((f32[4,8,8,512]{3,2,1,0:T(8,128)}, f32[4,8,8,512]{3,2,1,0:T(8,128)}, u32[]{:S(2)}, u32[]{:S(2)}) %collective-permute-start.9) | collective-permute-done | bytes 524320 | tf_op jit(solution)/shard_map/ppermute | solution.py:15
  173.7 10.5 %collective-permute-done.10 = f32[4,8,8,512]{3,2,1,0:T(8,128)S(1)} collective-permute-done((f32[4,8,8,512]{3,2,1,0:T(8,128)}, f32[4,8,8,512]{3,2,1,0:T(8,128)S(1)}, u32[]{:S(2)}, u32[]{:S(2)}) %collective-permute-start.10) | collective-permute-done | bytes 524320 | tf_op jit(solution)/shard_map/ppermute | solution.py:15
  184.2 0.7 collective-permute-start.11
  185.3 8.1 %collective-permute-done.11 = f32[4,8,8,512]{3,2,1,0:T(8,128)S(1)} collective-permute-done((f32[4,8,8,512]{3,2,1,0:T(8,128)S(1)}, f32[4,8,8,512]{3,2,1,0:T(8,128)S(1)}, u32[]{:S(2)}, u32[]{:S(2)}) %collective-permute-start.11) | collective-permute-done | bytes 524320 | tf_op jit(solution)/shard_map/ppermute | solution.py:15
  193.4 0.5 pad_select_fusion.1
  193.9 5.8 %fusion.150 = (f32[4,512]{1,0:T(4,128)S(1)}, f32[4,8,8,512]{3,2,1,0:T(8,128)S(1)}, f32[4,8,8,512]{3,2,1,0:T(8,128)}) fusion(f32[7,4,8,8,512]{4,3,2,1,0:T(8,128)S(1)} %pad_select_fusion.1, pred[]{:T(512)S(6)} %lt.13, bf16[4,8,8,4608]{3,2,1,0:T(8,128)(2,1)S(1)} %fusion.122, bf16[1,2,4608,512]{3,2,1,0:T(8,128)(2,1)} %param.9), kind=kOutput, calls=%fused_computation.282 | convolution fusion | flops 1208219648 | bytes 8658945 | tf_op jit(solution)/shard_map/dot_general | solution.py:45
  201.5 0.5 copy-done.11
  201.9 4.7 %bitcast_dynamic-update-slice_fusion.1 = (f32[5,4,8,8,512]{4,3,2,1,0:T(8,128)}, f32[4,8,8,512]{3,2,1,0:T(8,128)}) fusion(f32[5,4,8,8,512]{4,3,2,1,0:T(8,128)} %get-tuple-element.31, f32[4,8,8,512]{3,2,1,0:T(8,128)S(1)} %copy-done.11, pred[]{:T(512)S(6)} %lt.13, f32[4,8,8,512]{3,2,1,0:T(8,128)S(1)} %get-tuple-element.9, ...), kind=kOutput, calls=%fused_computation.136 | convolution fusion | flops 1208352768 | bytes 9175041 | tf_op jit(solution)/shard_map/dot_general | solution.py:45
  206.6 1.9 collective-permute-start.12
  208.5 2.1 collective-permute-start.13
  210.6 11.8 %collective-permute-done.12 = f32[4,8,8,512]{3,2,1,0:T(8,128)S(1)} collective-permute-done((f32[4,8,8,512]{3,2,1,0:T(8,128)}, f32[4,8,8,512]{3,2,1,0:T(8,128)S(1)}, u32[]{:S(2)}, u32[]{:S(2)}) %collective-permute-start.12) | collective-permute-done | bytes 524320 | tf_op jit(solution)/shard_map/ppermute | solution.py:21
  223.4 5.8 %collective-permute-done.13 = f32[4,8,8,512]{3,2,1,0:T(8,128)} collective-permute-done((f32[4,8,8,512]{3,2,1,0:T(8,128)}, f32[4,8,8,512]{3,2,1,0:T(8,128)}, u32[]{:S(2)}, u32[]{:S(2)}) %collective-permute-start.13) | collective-permute-done | bytes 524320 | tf_op jit(solution)/shard_map/ppermute | solution.py:15
  229.7 10.5 %collective-permute-done.14 = f32[4,8,8,512]{3,2,1,0:T(8,128)S(1)} collective-permute-done((f32[4,8,8,512]{3,2,1,0:T(8,128)}, f32[4,8,8,512]{3,2,1,0:T(8,128)S(1)}, u32[]{:S(2)}, u32[]{:S(2)}) %collective-permute-start.14) | collective-permute-done | bytes 524320 | tf_op jit(solution)/shard_map/ppermute | solution.py:15
  240.1 0.7 collective-permute-start.15
  241.2 8.1 %collective-permute-done.15 = f32[4,8,8,512]{3,2,1,0:T(8,128)S(1)} collective-permute-done((f32[4,8,8,512]{3,2,1,0:T(8,128)S(1)}, f32[4,8,8,512]{3,2,1,0:T(8,128)S(1)}, u32[]{:S(2)}, u32[]{:S(2)}) %collective-permute-start.15) | collective-permute-done | bytes 524320 | tf_op jit(solution)/shard_map/ppermute | solution.py:15
  249.3 0.5 pad_select_fusion
  249.9 5.1 %fusion.147 = (f32[4,512]{1,0:T(4,128)S(1)}, f32[4,8,8,512]{3,2,1,0:T(8,128)S(1)}, f32[4,8,8,512]{3,2,1,0:T(8,128)S(1)}) fusion(f32[7,4,8,8,512]{4,3,2,1,0:T(8,128)S(1)} %pad_select_fusion, pred[]{:T(512)S(6)} %lt.13, bf16[4,8,8,4608]{3,2,1,0:T(8,128)(2,1)S(1)} %fusion.138, bf16[1,2,4608,512]{3,2,1,0:T(8,128)(2,1)} %param.9), kind=kOutput, calls=%fused_computation.280 | convolution fusion | flops 1208219648 | bytes 8658945 | tf_op jit(solution)/shard_map/dot_general | solution.py:45
  256.6 4.5 %bitcast_dynamic-update-slice_fusion = (f32[5,4,8,8,512]{4,3,2,1,0:T(8,128)}, f32[4,8,8,512]{3,2,1,0:T(8,128)S(1)}) fusion(f32[5,4,8,8,512]{4,3,2,1,0:T(8,128)} %get-tuple-element.34, f32[4,8,8,512]{3,2,1,0:T(8,128)S(1)} %get-tuple-element.36, pred[]{:T(512)S(6)} %lt.13, f32[4,8,8,512]{3,2,1,0:T(8,128)S(1)} %get-tuple-element.5, ...), kind=kOutput, calls=%fused_computation.134 | convolution fusion | flops 1208352768 | bytes 9175041 | tf_op jit(solution)/shard_map/dot_general | solution.py:45
  261.1 9.2 %collective-permute-done.16 = f32[4,8,8,512]{3,2,1,0:T(8,128)S(1)} collective-permute-done((f32[4,8,8,512]{3,2,1,0:T(8,128)S(1)}, f32[4,8,8,512]{3,2,1,0:T(8,128)S(1)}, u32[]{:S(2)}, u32[]{:S(2)}) %collective-permute-start.16) | collective-permute-done | bytes 524320 | tf_op jit(solution)/shard_map/ppermute | solution.py:15
  270.3 10.7 %collective-permute-done.17 = f32[4,8,8,512]{3,2,1,0:T(8,128)S(1)} collective-permute-done((f32[4,8,8,512]{3,2,1,0:T(8,128)S(1)}, f32[4,8,8,512]{3,2,1,0:T(8,128)S(1)}, u32[]{:S(2)}, u32[]{:S(2)}) %collective-permute-start.17) | collective-permute-done | bytes 524320 | tf_op jit(solution)/shard_map/ppermute | solution.py:15
  281.0 0.7 collective-permute-start.18
  281.7 8.5 %collective-permute-done.18 = f32[4,8,8,512]{3,2,1,0:T(8,128)S(1)} collective-permute-done((f32[4,8,8,512]{3,2,1,0:T(8,128)S(1)}, f32[4,8,8,512]{3,2,1,0:T(8,128)S(1)}, u32[]{:S(2)}, u32[]{:S(2)}) %collective-permute-start.18) | collective-permute-done | bytes 524320 | tf_op jit(solution)/shard_map/ppermute | solution.py:15
  290.2 2.4 select_bitcast_fusion
  (241 shorter events, 15.3 us)
Async XLA Ops:
  0.6 6.0 %copy-start.4 = (f32[1,4,8,8,512]{4,3,2,1,0:T(8,128)S(1)}, f32[1,4,8,8,512]{4,3,2,1,0:T(8,128)}, u32[]{:S(2)}) copy-start(f32[1,4,8,8,512]{4,3,2,1,0:T(8,128)} %param.6) | copy-start | bytes 1572868
  7.0 1.4 copy-start.8
  19.4 17.0 %collective-permute-start = (f32[4,8,8,512]{3,2,1,0:T(8,128)}, f32[4,8,8,512]{3,2,1,0:T(8,128)}, u32[]{:S(2)}, u32[]{:S(2)}) collective-permute-start(f32[4,8,8,512]{3,2,1,0:T(8,128)} %get-tuple-element.26), channel_id=1, source_target_pairs={{0,32},{32,64},{64,96},{96,128},{128,160},{160,192},{192,224},{1,3... | collective-permute-start | bytes 1572872 | tf_op jit(solution)/shard_map/ppermute | solution.py:21
  22.8 23.6 %collective-permute-start.1 = (f32[4,8,8,512]{3,2,1,0:T(8,128)}, f32[4,8,8,512]{3,2,1,0:T(8,128)}, u32[]{:S(2)}, u32[]{:S(2)}) collective-permute-start(f32[4,8,8,512]{3,2,1,0:T(8,128)} %get-tuple-element.26), channel_id=1, source_target_pairs={{0,32},{32,0},{64,96},{96,64},{128,160},{160,128},{192,224},{224,1... | collective-permute-start | bytes 1572872 | tf_op jit(solution)/shard_map/ppermute | solution.py:15
  40.4 21.6 %copy-start.5 = (f32[4,8,8,512]{3,2,1,0:T(8,128)S(1)}, f32[4,8,8,512]{3,2,1,0:T(8,128)}, u32[]{:S(2)}) copy-start(f32[4,8,8,512]{3,2,1,0:T(8,128)} %get-tuple-element.17) | copy-start | bytes 1572868
  46.5 14.5 %collective-permute-start.2 = (f32[4,8,8,512]{3,2,1,0:T(8,128)}, f32[4,8,8,512]{3,2,1,0:T(8,128)S(1)}, u32[]{:S(2)}, u32[]{:S(2)}) collective-permute-start(f32[4,8,8,512]{3,2,1,0:T(8,128)} %collective-permute-done.1), channel_id=1, source_target_pairs={{0,64},{32,96},{64,0},{96,32},{128,192},{160,224},{192,128},{224,1... | collective-permute-start | bytes 1572872 | tf_op jit(solution)/shard_map/ppermute | solution.py:15
  61.0 11.9 %collective-permute-start.3 = (f32[4,8,8,512]{3,2,1,0:T(8,128)S(1)}, f32[4,8,8,512]{3,2,1,0:T(8,128)S(1)}, u32[]{:S(2)}, u32[]{:S(2)}) collective-permute-start(f32[4,8,8,512]{3,2,1,0:T(8,128)S(1)} %collective-permute-done.2), channel_id=1, source_target_pairs={{0,128},{32,160},{64,192},{96,224},{128,0},{160,32},{192,64},{224,... | collective-permute-start | bytes 1572872 | tf_op jit(solution)/shard_map/ppermute | solution.py:15
  73.5 5.9 %copy-start.1 = (f32[7,4,8,8,512]{4,3,2,1,0:T(8,128)}, f32[7,4,8,8,512]{4,3,2,1,0:T(8,128)S(1)}, u32[]{:S(2)}) copy-start(f32[7,4,8,8,512]{4,3,2,1,0:T(8,128)S(1)} %pad_select_fusion.3) | copy-start | bytes 11010052
  80.5 1.0 copy-start.6
  80.5 1.2 copy-start.9
  86.3 17.1 %copy-start.7 = (f32[4,4,8,8,512]{4,3,2,1,0:T(8,128)S(1)}, f32[4,4,8,8,512]{4,3,2,1,0:T(8,128)}, u32[]{:S(2)}) copy-start(f32[4,4,8,8,512]{4,3,2,1,0:T(8,128)} %param.7) | copy-start | bytes 6291460
  86.3 17.1 %collective-permute-start.4 = (f32[4,8,8,512]{3,2,1,0:T(8,128)}, f32[4,8,8,512]{3,2,1,0:T(8,128)S(1)}, u32[]{:S(2)}, u32[]{:S(2)}) collective-permute-start(f32[4,8,8,512]{3,2,1,0:T(8,128)} %get-tuple-element.29), channel_id=1, source_target_pairs={{0,32},{32,64},{64,96},{96,128},{128,160},{160,192},{192,224},{1,3... | collective-permute-start | bytes 1572872 | tf_op jit(solution)/shard_map/ppermute | solution.py:21
  88.8 22.5 %collective-permute-start.5 = (f32[4,8,8,512]{3,2,1,0:T(8,128)}, f32[4,8,8,512]{3,2,1,0:T(8,128)}, u32[]{:S(2)}, u32[]{:S(2)}) collective-permute-start(f32[4,8,8,512]{3,2,1,0:T(8,128)} %get-tuple-element.29), channel_id=1, source_target_pairs={{0,32},{32,0},{64,96},{96,64},{128,160},{160,128},{192,224},{224,1... | collective-permute-start | bytes 1572872 | tf_op jit(solution)/shard_map/ppermute | solution.py:15
  111.3 11.9 %collective-permute-start.6 = (f32[4,8,8,512]{3,2,1,0:T(8,128)}, f32[4,8,8,512]{3,2,1,0:T(8,128)S(1)}, u32[]{:S(2)}, u32[]{:S(2)}) collective-permute-start(f32[4,8,8,512]{3,2,1,0:T(8,128)} %collective-permute-done.5), channel_id=1, source_target_pairs={{0,64},{32,96},{64,0},{96,32},{128,192},{160,224},{192,128},{224,1... | collective-permute-start | bytes 1572872 | tf_op jit(solution)/shard_map/ppermute | solution.py:15
  116.1 16.3 %slice-start.1 = ((f32[7,4,8,8,512]{4,3,2,1,0:T(8,128)}), f32[6,4,8,8,512]{4,3,2,1,0:T(8,128)S(1)}, s32[]{:S(2)}) async-start(f32[7,4,8,8,512]{4,3,2,1,0:T(8,128)} %copy-done.1), calls=%async_computation.1 | async-start | bytes 6291456 | tf_op jit(solution)/shard_map/slice | solution.py:81
  123.2 9.2 %collective-permute-start.7 = (f32[4,8,8,512]{3,2,1,0:T(8,128)S(1)}, f32[4,8,8,512]{3,2,1,0:T(8,128)S(1)}, u32[]{:S(2)}, u32[]{:S(2)}) collective-permute-start(f32[4,8,8,512]{3,2,1,0:T(8,128)S(1)} %collective-permute-done.6), channel_id=1, source_target_pairs={{0,128},{32,160},{64,192},{96,224},{128,0},{160,32},{192,64},{224,... | collective-permute-start | bytes 1572872 | tf_op jit(solution)/shard_map/ppermute | solution.py:15
  132.9 5.9 %copy-start.2 = (f32[7,4,8,8,512]{4,3,2,1,0:T(8,128)}, f32[7,4,8,8,512]{4,3,2,1,0:T(8,128)S(1)}, u32[]{:S(2)}) copy-start(f32[7,4,8,8,512]{4,3,2,1,0:T(8,128)S(1)} %pad_select_fusion.2) | copy-start | bytes 11010052
  139.9 1.0 copy-start.10
  145.6 17.2 %collective-permute-start.8 = (f32[4,8,8,512]{3,2,1,0:T(8,128)}, f32[4,8,8,512]{3,2,1,0:T(8,128)S(1)}, u32[]{:S(2)}, u32[]{:S(2)}) collective-permute-start(f32[4,8,8,512]{3,2,1,0:T(8,128)} %get-tuple-element.32), channel_id=1, source_target_pairs={{0,32},{32,64},{64,96},{96,128},{128,160},{160,192},{192,224},{1,3... | collective-permute-start | bytes 1572872 | tf_op jit(solution)/shard_map/ppermute | solution.py:21
  149.1 24.2 %collective-permute-start.9 = (f32[4,8,8,512]{3,2,1,0:T(8,128)}, f32[4,8,8,512]{3,2,1,0:T(8,128)}, u32[]{:S(2)}, u32[]{:S(2)}) collective-permute-start(f32[4,8,8,512]{3,2,1,0:T(8,128)} %get-tuple-element.32), channel_id=1, source_target_pairs={{0,32},{32,0},{64,96},{96,64},{128,160},{160,128},{192,224},{224,1... | collective-permute-start | bytes 1572872 | tf_op jit(solution)/shard_map/ppermute | solution.py:15
  173.3 10.9 %collective-permute-start.10 = (f32[4,8,8,512]{3,2,1,0:T(8,128)}, f32[4,8,8,512]{3,2,1,0:T(8,128)S(1)}, u32[]{:S(2)}, u32[]{:S(2)}) collective-permute-start(f32[4,8,8,512]{3,2,1,0:T(8,128)} %collective-permute-done.9), channel_id=1, source_target_pairs={{0,64},{32,96},{64,0},{96,32},{128,192},{160,224},{192,128},{224,1... | collective-permute-start | bytes 1572872 | tf_op jit(solution)/shard_map/ppermute | solution.py:15
  173.6 19.8 %slice-start.2 = ((f32[7,4,8,8,512]{4,3,2,1,0:T(8,128)}), f32[6,4,8,8,512]{4,3,2,1,0:T(8,128)S(1)}, s32[]{:S(2)}) async-start(f32[7,4,8,8,512]{4,3,2,1,0:T(8,128)} %copy-done.2), calls=%async_computation.2 | async-start | bytes 6291456 | tf_op jit(solution)/shard_map/slice | solution.py:81
  184.2 9.2 %collective-permute-start.11 = (f32[4,8,8,512]{3,2,1,0:T(8,128)S(1)}, f32[4,8,8,512]{3,2,1,0:T(8,128)S(1)}, u32[]{:S(2)}, u32[]{:S(2)}) collective-permute-start(f32[4,8,8,512]{3,2,1,0:T(8,128)S(1)} %collective-permute-done.10), channel_id=1, source_target_pairs={{0,128},{32,160},{64,192},{96,224},{128,0},{160,32},{192,64},{224,... | collective-permute-start | bytes 1572872 | tf_op jit(solution)/shard_map/ppermute | solution.py:15
  193.9 5.9 %copy-start.3 = (f32[7,4,8,8,512]{4,3,2,1,0:T(8,128)}, f32[7,4,8,8,512]{4,3,2,1,0:T(8,128)S(1)}, u32[]{:S(2)}) copy-start(f32[7,4,8,8,512]{4,3,2,1,0:T(8,128)S(1)} %pad_select_fusion.1) | copy-start | bytes 11010052
  200.9 1.0 copy-start.11
  206.6 15.8 %collective-permute-start.12 = (f32[4,8,8,512]{3,2,1,0:T(8,128)}, f32[4,8,8,512]{3,2,1,0:T(8,128)S(1)}, u32[]{:S(2)}, u32[]{:S(2)}) collective-permute-start(f32[4,8,8,512]{3,2,1,0:T(8,128)} %get-tuple-element.35), channel_id=1, source_target_pairs={{0,32},{32,64},{64,96},{96,128},{128,160},{160,192},{192,224},{1,3... | collective-permute-start | bytes 1572872 | tf_op jit(solution)/shard_map/ppermute | solution.py:21
  208.5 20.7 %collective-permute-start.13 = (f32[4,8,8,512]{3,2,1,0:T(8,128)}, f32[4,8,8,512]{3,2,1,0:T(8,128)}, u32[]{:S(2)}, u32[]{:S(2)}) collective-permute-start(f32[4,8,8,512]{3,2,1,0:T(8,128)} %get-tuple-element.35), channel_id=1, source_target_pairs={{0,32},{32,0},{64,96},{96,64},{128,160},{160,128},{192,224},{224,1... | collective-permute-start | bytes 1572872 | tf_op jit(solution)/shard_map/ppermute | solution.py:15
  229.2 10.9 %collective-permute-start.14 = (f32[4,8,8,512]{3,2,1,0:T(8,128)}, f32[4,8,8,512]{3,2,1,0:T(8,128)S(1)}, u32[]{:S(2)}, u32[]{:S(2)}) collective-permute-start(f32[4,8,8,512]{3,2,1,0:T(8,128)} %collective-permute-done.13), channel_id=1, source_target_pairs={{0,64},{32,96},{64,0},{96,32},{128,192},{160,224},{192,128},{224,1... | collective-permute-start | bytes 1572872 | tf_op jit(solution)/shard_map/ppermute | solution.py:15
  229.5 19.8 %slice-start.3 = ((f32[7,4,8,8,512]{4,3,2,1,0:T(8,128)}), f32[6,4,8,8,512]{4,3,2,1,0:T(8,128)S(1)}, s32[]{:S(2)}) async-start(f32[7,4,8,8,512]{4,3,2,1,0:T(8,128)} %copy-done.3), calls=%async_computation.3 | async-start | bytes 6291456 | tf_op jit(solution)/shard_map/slice | solution.py:81
  240.1 9.2 %collective-permute-start.15 = (f32[4,8,8,512]{3,2,1,0:T(8,128)S(1)}, f32[4,8,8,512]{3,2,1,0:T(8,128)S(1)}, u32[]{:S(2)}, u32[]{:S(2)}) collective-permute-start(f32[4,8,8,512]{3,2,1,0:T(8,128)S(1)} %collective-permute-done.14), channel_id=1, source_target_pairs={{0,128},{32,160},{64,192},{96,224},{128,0},{160,32},{192,64},{224,... | collective-permute-start | bytes 1572872 | tf_op jit(solution)/shard_map/ppermute | solution.py:15
  249.8 5.1 %copy-start = (f32[7,4,8,8,512]{4,3,2,1,0:T(8,128)}, f32[7,4,8,8,512]{4,3,2,1,0:T(8,128)S(1)}, u32[]{:S(2)}) copy-start(f32[7,4,8,8,512]{4,3,2,1,0:T(8,128)S(1)} %pad_select_fusion) | copy-start | bytes 11010052
  261.1 9.2 %collective-permute-start.16 = (f32[4,8,8,512]{3,2,1,0:T(8,128)S(1)}, f32[4,8,8,512]{3,2,1,0:T(8,128)S(1)}, u32[]{:S(2)}, u32[]{:S(2)}) collective-permute-start(f32[4,8,8,512]{3,2,1,0:T(8,128)S(1)} %get-tuple-element.38), channel_id=1, source_target_pairs={{0,32},{32,0},{64,96},{96,64},{128,160},{160,128},{192,224},{224,1... | collective-permute-start | bytes 1572872 | tf_op jit(solution)/shard_map/ppermute | solution.py:15
  270.3 10.7 %collective-permute-start.17 = (f32[4,8,8,512]{3,2,1,0:T(8,128)S(1)}, f32[4,8,8,512]{3,2,1,0:T(8,128)S(1)}, u32[]{:S(2)}, u32[]{:S(2)}) collective-permute-start(f32[4,8,8,512]{3,2,1,0:T(8,128)S(1)} %collective-permute-done.16), channel_id=1, source_target_pairs={{0,64},{32,96},{64,0},{96,32},{128,192},{160,224},{192,128},{224,1... | collective-permute-start | bytes 1572872 | tf_op jit(solution)/shard_map/ppermute | solution.py:15
  281.0 9.2 %collective-permute-start.18 = (f32[4,8,8,512]{3,2,1,0:T(8,128)S(1)}, f32[4,8,8,512]{3,2,1,0:T(8,128)S(1)}, u32[]{:S(2)}, u32[]{:S(2)}) collective-permute-start(f32[4,8,8,512]{3,2,1,0:T(8,128)S(1)} %collective-permute-done.17), channel_id=1, source_target_pairs={{0,128},{32,160},{64,192},{96,224},{128,0},{160,32},{192,64},{224,... | collective-permute-start | bytes 1572872 | tf_op jit(solution)/shard_map/ppermute | solution.py:15
  281.7 8.5 %slice-start = ((f32[7,4,8,8,512]{4,3,2,1,0:T(8,128)}), f32[6,4,8,8,512]{4,3,2,1,0:T(8,128)S(1)}, s32[]{:S(2)}) async-start(f32[7,4,8,8,512]{4,3,2,1,0:T(8,128)} %copy-done), calls=%async_computation | async-start | bytes 6291456 | tf_op jit(solution)/shard_map/slice | solution.py:81
where the time goes:
time: 294 us; the launch traced here: 293 us
  waiting for transfers between devices  178 us (61%)
  matrix products  50.4 us (17%)
  starting transfers between devices  27.7 us (9%)
  other arithmetic  18.6 us (6%)
  local copies, waits for them, and re-layouts  16.2 us (6%)
    ppermute x15, waiting for transfers between devices, from_partner(): return lax.ppermute(value, axis, pairs)  130 us
    dot_general x10, matrix products, convolve(): jnp.dot(patches.reshape(images * height_cells * width_cells, 9 * channels...  50.4 us
    ppermute x4, waiting for transfers between devices, from_behind(): return lax.ppermute(array, axis, pairs)  48 us
    ppermute x15, starting transfers between devices, from_partner(): return lax.ppermute(value, axis, pairs)  16.4 us
    ppermute x4, starting transfers between devices, from_behind(): return lax.ppermute(array, axis, pairs)  11.3 us
    unnamed x94, local copies, waits for them, and re-layouts  6.33 us
  transfers between devices with their start and end apart: 19, of which 19 were waited for; matrix products, arithmetic and copies ran while one was open for 4% of the time, Pallas kernels for 0%

commit v1 on v0

v1 whole, which is shorter than its diff:
```python
import functools

import jax
import jax.numpy as jnp
from jax import lax
from jax.experimental import pallas as pl
from jax.experimental.pallas import tpu as pltpu
from jax.sharding import PartitionSpec as P

MESH = pl.DeviceIdType.MESH
GROUP = 16
EPS = 1e-05
SIDE = 8
CELLS = SIDE * SIDE
LAG = 2


def group_stats(x):
    cells, channels = x.shape
    mean = jnp.mean(x, axis=0, keepdims=True)
    spread = jnp.mean(jnp.square(x - mean), axis=0, keepdims=True)
    lane = lax.broadcasted_iota(jnp.int32, (1, channels), 1)
    for step in (1, 2, 4, 8):
        upper = (lane & step) != 0
        other_mean = jnp.where(upper, pltpu.roll(mean, step, 1), pltpu.roll(mean, channels - step, 1))
        other_spread = jnp.where(upper, pltpu.roll(spread, step, 1), pltpu.roll(spread, channels - step, 1))
        half = 0.5 * (mean - other_mean)
        mean = 0.5 * (mean + other_mean)
        spread = 0.5 * (spread + other_spread) + half * half
    return mean, spread


def fill_patches(x, gain, shift, patches):
    cells, channels = x.shape
    mean, spread = group_stats(x)
    u = (x - mean) * lax.rsqrt(spread + EPS) * gain + shift
    a = u / (1.0 + jnp.exp(-u))
    column = lax.broadcasted_iota(jnp.int32, (cells, channels), 0) % SIDE
    edge = jnp.zeros((SIDE, channels), jnp.float32)
    for c in range(3):
        if c == 0:
            moved = jnp.where(column == 0, 0.0, pltpu.roll(a, 1, 0))
        elif c == 2:
            moved = jnp.where(column == SIDE - 1, 0.0, pltpu.roll(a, cells - 1, 0))
        else:
            moved = a
        for r in range(3):
            if r == 0:
                rows = jnp.concatenate([edge, moved[:-SIDE]], axis=0)
            elif r == 2:
                rows = jnp.concatenate([moved[SIDE:], edge], axis=0)
            else:
                rows = moved
            k = 3 * r + c
            patches[:, k * channels : (k + 1) * channels] = rows.astype(jnp.bfloat16)


def window(
    images,
    ticks,
    handoff,
    fresh,
    skips,
    weights,
    gain,
    shift,
    act,
    queue,
    w,
    x_in,
    out_v,
    mirror,
    q,
    feed,
    patches,
    load_sem,
    hand_send,
    hand_recv,
    mir_send,
    mir_recv,
    rel_send,
    out_sem,
):
    s = lax.axis_index("segment")
    sections = 8
    steps = images * ticks
    handed = images * (ticks - 1)
    encoder = s < sections // 2

    load_x = pltpu.make_async_copy(handoff, x_in.at[pl.ds(0, images)], load_sem.at[0])
    load_w = [pltpu.make_async_copy(weights.at[k], w.at[k], load_sem.at[1 + k]) for k in range(2)]
    load_fresh = pltpu.make_async_copy(fresh, x_in.at[pl.ds(images, handed)], load_sem.at[3])
    load_q = pltpu.make_async_copy(skips.at[pl.ds(0, steps)], q, load_sem.at[4])
    keep_q = pltpu.make_async_copy(
        skips.at[pl.ds(steps, 2 * images)], queue.at[pl.ds(0, 2 * images)], load_sem.at[5]
    )
    load_x.start()
    load_w[0].start()
    load_w[1].start()
    pl.when(s == 0)(load_fresh.start)
    pl.when(s >= sections // 2)(load_q.start)
    pl.when(s == sections - 1)(keep_q.start)

    barrier = pltpu.get_barrier_semaphore()
    for k in range(1, sections):
        pl.semaphore_signal(barrier, 1, device_id={"segment": lax.rem(s + k, sections)}, device_id_type=MESH)
    pl.semaphore_wait(barrier, sections - 1)

    def hand(n):
        return pltpu.make_async_remote_copy(
            out_v.at[n],
            x_in.at[n + images],
            hand_send.at[n],
            hand_recv.at[n + images],
            device_id={"segment": jnp.minimum(s + 1, sections - 1)},
            device_id_type=MESH,
        )

    def hand_arrived(n):
        pltpu.make_async_remote_copy(
            out_v.at[n],
            x_in.at[n],
            hand_send.at[n],
            hand_recv.at[n],
            device_id={"segment": jnp.minimum(s + 1, sections - 1)},
            device_id_type=MESH,
        ).wait_recv()

    def to_mirror(source, n, sem, target):
        return pltpu.make_async_remote_copy(
            source, mirror.at[n], sem, mir_recv.at[n], device_id={"segment": target}, device_id_type=MESH
        )

    def to_queue(source, n, slot, sem, target):
        return pltpu.make_async_remote_copy(
            source, queue.at[slot], sem, mir_recv.at[n], device_id={"segment": target}, device_id_type=MESH
        )

    def relay(m):
        to_mirror(mirror.at[m], m, rel_send.at[m], jnp.int32(1)).wait_recv()

        @pl.when(m < 2 * images)
        def _():
            to_mirror(mirror.at[m], m, rel_send.at[m], jnp.int32(5)).start()

        @pl.when(m >= 2 * images)
        def _():
            to_queue(mirror.at[m], m, m - 2 * images, rel_send.at[m], jnp.int32(5)).start()

    load_x.wait()
    load_w[0].wait()

    def step(n, carry):
        @pl.when((s == 0) & (n == images))
        def _():
            load_fresh.wait()

        @pl.when((s > 0) & (n >= images))
        def _():
            hand_arrived(n)

        @pl.when((s == 2) & (n >= images))
        def _():
            to_queue(x_in.at[n], n - images, n - images, rel_send.at[n - images], jnp.int32(6)).start()

        @pl.when((s == 1) & (n >= LAG) & (n < handed + LAG))
        def _():
            relay(n - LAG)

        @pl.when(n == 0)
        def _():
            load_w[1].wait()

        @pl.when((s >= sections // 2) & (n == 0))
        def _():
            load_q.wait()

        fill_patches(x_in[n], gain[0:1], shift[0:1], patches.at[0])
        first = jnp.dot(patches[0], w[0], preferred_element_type=jnp.float32)

        @pl.when(encoder)
        def _():
            feed[...] = first
            out_v[n] = x_in[n]

        @pl.when(jnp.logical_not(encoder))
        def _():
            out_v[n] = x_in[n] + first

        @pl.when((s == 4) & (n >= images))
        def _():
            feed[...] = x_in[n]

        @pl.when((s == 5) & (n >= 3 * images))
        def _():
            to_mirror(mirror.at[n - 3 * images], n - 3 * images, rel_send.at[n - 3 * images], jnp.int32(4)).wait_recv()
            feed[...] = mirror[n - 3 * images]

        @pl.when(
            ((s == 4) & (n < images)) | ((s == 5) & (n < 3 * images)) | (s >= 6)
        )
        def _():
            feed[...] = q[n]

        fill_patches(feed[...], gain[1:2], shift[1:2], patches.at[1])
        second = jnp.dot(patches[1], w[1], preferred_element_type=jnp.float32)
        out_v[n] = out_v[n] + second

        @pl.when((s < sections - 1) & (n < handed))
        def _():
            hand(n).start()

        @pl.when(s == 0)
        def _():
            to_queue(out_v.at[n], n, n + 2 * images, mir_send.at[n], jnp.int32(7)).start()

        @pl.when((s == 1) & (n >= handed))
        def _():
            to_queue(out_v.at[n], n, n, mir_send.at[n], jnp.int32(6)).start()

        @pl.when((s == 2) & (n < handed))
        def _():
            to_mirror(out_v.at[n], n, mir_send.at[n], jnp.int32(1)).start()

        @pl.when((s == 2) & (n >= handed))
        def _():
            to_queue(out_v.at[n], n, n - 2 * images, mir_send.at[n], jnp.int32(5)).start()

        @pl.when((s == 3) & (n >= handed))
        def _():
            to_queue(out_v.at[n], n, n - handed, mir_send.at[n], jnp.int32(4)).start()

        pltpu.make_async_copy(out_v.at[n], act.at[n], out_sem.at[n]).start()
        return carry

    lax.fori_loop(0, steps, step, 0)

    def drain(n, carry):
        @pl.when((s < sections - 1) & (n < handed))
        def _():
            hand(n).wait_send()

        @pl.when((s == 0) | (s == 2) | (((s == 1) | (s == 3)) & (n >= handed)))
        def _():
            to_mirror(out_v.at[n], n, mir_send.at[n], jnp.int32(7)).wait_send()

        @pl.when(((s == 1) | (s == 2)) & (n < handed))
        def _():
            to_mirror(out_v.at[n], n, rel_send.at[n], jnp.int32(6)).wait_send()

        @pl.when(((s == 4) & (n >= handed)) | ((s == 5) & (n >= 2 * images)) | (s >= 6))
        def _():
            to_queue(out_v.at[n], n, n, rel_send.at[n], jnp.int32(6)).wait_recv()

        pltpu.make_async_copy(out_v.at[n], act.at[n], out_sem.at[n]).wait()
        return carry

    lax.fori_loop(0, steps, drain, 0)
    pl.when(s == sections - 1)(keep_q.wait)


def per_device(handoff, fresh, skip_queue, conv_weight, norm_gain, norm_shift):
    _, images, height, width, channels = handoff.shape
    ticks = fresh.shape[0] + 1
    depth = skip_queue.shape[1]
    steps = images * ticks
    cells = height * width
    s = lax.axis_index("segment")
    f32 = jnp.float32
    anywhere = pl.BlockSpec(memory_space=pl.ANY)
    hbm = pl.BlockSpec(memory_space=pltpu.HBM)
    vmem = pl.BlockSpec(memory_space=pltpu.VMEM)
    act, queue = pl.pallas_call(
        functools.partial(window, images, ticks),
        out_shape=(
            jax.ShapeDtypeStruct((steps, cells, channels), f32),
            jax.ShapeDtypeStruct((images * depth, cells, channels), f32),
        ),
        in_specs=[hbm, hbm, hbm, hbm, vmem, vmem],
        out_specs=(anywhere, anywhere),
        scratch_shapes=[
            pltpu.VMEM((2, 9 * channels, channels), jnp.bfloat16),
            pltpu.VMEM((steps, cells, channels), f32),
            pltpu.VMEM((steps, cells, channels), f32),
            pltpu.VMEM((steps, cells, channels), f32),
            pltpu.VMEM((steps, cells, channels), f32),
            pltpu.VMEM((cells, channels), f32),
            pltpu.VMEM((2, cells, 9 * channels), jnp.bfloat16),
            pltpu.SemaphoreType.DMA((6,)),
            pltpu.SemaphoreType.DMA((steps,)),
            pltpu.SemaphoreType.DMA((steps,)),
            pltpu.SemaphoreType.DMA((steps,)),
            pltpu.SemaphoreType.DMA((steps,)),
            pltpu.SemaphoreType.DMA((steps,)),
            pltpu.SemaphoreType.DMA((steps,)),
        ],
        compiler_params=pltpu.CompilerParams(
            collective_id=0, has_side_effects=True, vmem_limit_bytes=36 << 20
        ),
        cost_estimate=pl.CostEstimate(
            flops=4 * steps * cells * 9 * channels * channels, bytes_accessed=20 << 20, transcendentals=0
        ),
        name="window",
    )(
        pltpu.with_memory_space_constraint(handoff.reshape(images, cells, channels), pltpu.HBM),
        pltpu.with_memory_space_constraint(fresh.reshape(steps - images, cells, channels), pltpu.HBM),
        pltpu.with_memory_space_constraint(skip_queue.reshape(images * depth, cells, channels), pltpu.HBM),
        pltpu.with_memory_space_constraint(conv_weight[0], pltpu.HBM),
        pltpu.with_memory_space_constraint(norm_gain[0], pltpu.HBM),
        pltpu.with_memory_space_constraint(norm_shift[0], pltpu.HBM),
    )
    filled = jnp.arange(depth) < jnp.where(s >= 4, 2 * s - 7, 0)
    queue = queue.reshape(depth, images, height, width, channels)
    queue = jnp.where(filled[:, None, None, None, None], queue, jnp.float32(0.0))
    return act.reshape(1, ticks, images, height, width, channels), queue[None]


def solution(mesh):
    return jax.shard_map(
        per_device,
        mesh=mesh,
        in_specs=(
            P("segment", "dp", None, None, None),
            P(None, "dp", None, None, None),
            P("segment", None, "dp", None, None, None),
            P("segment", None, None, None),
            P("segment", None, None),
            P("segment", None, None),
        ),
        out_specs=(
            P("segment", None, "dp", None, None, None),
            P("segment", None, "dp", None, None, None),
        ),
        check_vma=False,
    )
```

time: 294 us -> 81.9 us (0.28)
  waiting for transfers between devices: 178 us -> 0 us
  Pallas kernels: 0 us -> 77 us
  matrix products: 50.4 us -> 0 us
  starting transfers between devices: 27.7 us -> 0 us
  other arithmetic: 18.6 us -> 2.6 us
  local copies, waits for them, and re-layouts: 16.2 us -> 1.49 us
    ppermute x19 -> x0, waiting for transfers between devices: 178 us -> none  [the longest x15 130 us: from_partner(): return lax.ppermute(value, axis, pairs)]
    pallas_call x0 -> x1, Pallas kernels: none -> 77 us  [per_device(): pl.pallas_call(functools.partial(window, images, ticks), out_shape=(jax.S...]
    dot_general x10 -> x0, matrix products: 50.4 us -> none  [convolve(): jnp.dot(patches.reshape(images * height_cells * width_cells, 9 * channels...]
    ppermute x19 -> x0, starting transfers between devices: 27.7 us -> none  [the longest x15 16.4 us: from_partner(): return lax.ppermute(value, axis, pairs)]
    reduce_sum x35 -> x0, other arithmetic: 8.25 us -> none  [the longest x15 4.43 us: group_silu(): average = jnp.mean(grouped, axis=(1, 3), keepdims=True)]
    unnamed x94 -> x1, local copies, waits for them, and re-layouts: 6.33 us -> 1.49 us
    slice x11 -> x0, local copies, waits for them, and re-layouts: 3.87 us -> none  [the longest x9 2.33 us: per_device(): pending[1:]]
    convert_element_type x10 -> x0, other arithmetic: 3.85 us -> none  [group_silu(): return jax.nn.silu(scaled).astype(jnp.bfloat16)]
  transfers between devices with their start and end apart: 19 -> 0, of which waited for: 19 -> 0; matrix products, arithmetic and copies ran while one was open for 4% -> 0% of each run, Pallas kernels for 0% -> 0%
where the time goes in v1:
time: 81.9 us; the launch traced here: 81.7 us
  Pallas kernels  77 us (94%)
  other arithmetic  2.6 us (3%)
  local copies, waits for them, and re-layouts  1.49 us (2%)
    pallas_call x1, Pallas kernels, per_device(): pl.pallas_call(functools.partial(window, images, ticks), out_shape=(jax.S...  77 us
    select_n x1, other arithmetic, per_device(): jnp.where(filled[:, None, None, None, None], queue, jnp.float32(0.0))  2.59 us

profile of v1, /device:TPU:174, one launch (start us, length us, event | category | flops | bytes accessed | tf_op | source)
XLA Modules:
  0.0 81.7 jit_solution(2402193513312474726)
XLA Ops:
  0.7 77.0 %window.1 = (f32[20,64,512]{2,1,0:T(8,128)S(1)}, f32[28,64,512]{2,1,0:T(8,128)S(1)}) custom-call(f32[4,64,512]{2,1,0:T(8,128)} %bitcast.13, f32[16,64,512]{2,1,0:T(8,128)} %bitcast.12, f32[28,64,512]{2,1,0:T(8,128)} %bitcast.11, bf16[2,4608,512]{2,1,0:T(8,128)(2,1)} %bitcast.10, f32[2,512]{1,0:T(2,128)} %bitcast.14, f32[2,512]{1,0:T(2,128)} %bitcast.15), custom_call_target="tpu_custom_call" | custom-call | flops 12079595520 | bytes 20971520 | tf_op jit(solution)/shard_map/window/pallas_call | solution.py:273
  77.6 2.6 %broadcast_select_fusion = f32[1,7,4,8,8,512]{5,4,3,2,1,0:T(8,128)} fusion(f32[1,7,4,8,8,512]{5,4,3,2,1,0:T(8,128)S(1)} %bitcast.8, pred[7]{0:T(512)(128)(4,1)S(1)} %iota_compare_fusion), kind=kLoop, calls=%fused_computation | loop fusion | flops 917504 | bytes 7340039 | tf_op jit(solution)/shard_map/jit(_where)/select_n | solution.py:314
  80.2 1.5 %copy.9 = f32[1,5,4,8,8,512]{5,4,3,2,1,0:T(8,128)} copy(f32[1,5,4,8,8,512]{5,4,3,2,1,0:T(8,128)S(1)} %bitcast.9) | data formatting | bytes 5242880
  (1 shorter events, 0.0 us)

commit v2 on v0

v2 whole, which is shorter than its diff:
```python
import functools

import jax
import jax.numpy as jnp
from jax import lax
from jax.experimental import pallas as pl
from jax.experimental.pallas import tpu as pltpu
from jax.sharding import PartitionSpec as P

MESH = pl.DeviceIdType.MESH
EPS = 1e-05
SIDE = 8
LANES = 128
PAIR = 2
SECTIONS = 8


def merge_four(mean, spread, step):
    lane = lax.broadcasted_iota(jnp.int32, mean.shape, 1)
    digit = (lane // step) % 4

    def around(v):
        others = []
        for k in range(1, 4):
            ahead = pltpu.roll(v, LANES - k * step, 1)
            behind = pltpu.roll(v, (4 - k) * step, 1)
            others.append(jnp.where(digit < 4 - k, ahead, behind))
        return [v] + others

    means = around(mean)
    spreads = around(spread)
    mean = 0.25 * ((means[0] + means[1]) + (means[2] + means[3]))
    between = [jnp.square(m - mean) for m in means]
    spread = 0.25 * (
        ((spreads[0] + between[0]) + (spreads[1] + between[1]))
        + ((spreads[2] + between[2]) + (spreads[3] + between[3]))
    )
    return mean, spread


def fill_patches(x, gain, shift, patches):
    images, cells, channels = x.shape
    column = lax.broadcasted_iota(jnp.int32, (cells, LANES), 0) % SIDE
    edge = jnp.zeros((SIDE, LANES), jnp.float32)
    for lo in range(0, channels, LANES):
        part = x[:, :, lo : lo + LANES]
        mean = jnp.mean(part, axis=1)
        spread = jnp.mean(jnp.square(part - mean[:, None]), axis=1)
        for step in (1, 4):
            mean, spread = merge_four(mean, spread, step)
        scale = lax.rsqrt(spread + EPS) * gain[:, lo : lo + LANES]
        for image in range(images):
            u = (part[image] - mean[image : image + 1]) * scale[image : image + 1] + shift[:, lo : lo + LANES]
            a = u / (1.0 + jnp.exp(-u))
            for c in range(3):
                if c == 0:
                    moved = jnp.where(column == 0, 0.0, pltpu.roll(a, 1, 0))
                elif c == 2:
                    moved = jnp.where(column == SIDE - 1, 0.0, pltpu.roll(a, cells - 1, 0))
                else:
                    moved = a
                for r in range(3):
                    if r == 0:
                        rows = jnp.concatenate([edge, moved[:-SIDE]], axis=0)
                    elif r == 2:
                        rows = jnp.concatenate([moved[SIDE:], edge], axis=0)
                    else:
                        rows = moved
                    at = (3 * r + c) * channels + lo
                    patches[image * cells : (image + 1) * cells, at : at + LANES] = rows.astype(jnp.bfloat16)


def window(
    images,
    ticks,
    handoff,
    fresh,
    skips,
    weights,
    gains,
    shifts,
    act,
    queue,
    w,
    gain,
    shift,
    bank,
    out_v,
    patches,
    load_sem,
    hand_send,
    hand_recv,
    mir_send,
    mir_recv,
    rel_send,
    out_sem,
):
    s = lax.axis_index("segment")
    steps = images * ticks
    handed = images * (ticks - 1)
    pairs = steps // PAIR
    half = SECTIONS // 2
    encoder = s < half
    cells, channels = bank.shape[1:]
    side = steps
    spare = 2 * steps

    load_x = pltpu.make_async_copy(handoff, bank.at[pl.ds(0, images)], load_sem.at[0])
    load_w = [pltpu.make_async_copy(weights.at[k], w.at[k], load_sem.at[1 + k]) for k in range(2)]
    load_fresh = pltpu.make_async_copy(fresh, bank.at[pl.ds(images, handed)], load_sem.at[3])
    keep_q = pltpu.make_async_copy(
        skips.at[pl.ds(steps, 2 * images)], queue.at[pl.ds(0, 2 * images)], load_sem.at[5]
    )
    load_gain = pltpu.make_async_copy(gains, gain, load_sem.at[6])
    load_shift = pltpu.make_async_copy(shifts, shift, load_sem.at[7])

    def load_q(count):
        return pltpu.make_async_copy(
            skips.at[pl.ds(0, count)], bank.at[pl.ds(side, count)], load_sem.at[4]
        )

    own_skips = ((s == half, images), (s == half + 1, 3 * images), (s >= half + 2, steps))
    load_gain.start()
    load_shift.start()
    load_x.start()
    for here, count in own_skips:
        pl.when(here)(load_q(count).start)

    @pl.when(encoder)
    def _():
        load_w[0].start()
        load_w[1].start()

    @pl.when(jnp.logical_not(encoder))
    def _():
        load_w[1].start()
        load_w[0].start()

    pl.when(s == 0)(load_fresh.start)
    pl.when(s == SECTIONS - 1)(keep_q.start)

    barrier = pltpu.get_barrier_semaphore()
    for k in range(1, SECTIONS):
        pl.semaphore_signal(barrier, 1, device_id={"segment": lax.rem(s + k, SECTIONS)}, device_id_type=MESH)

    def to_bank(source, slot, send, recv, target):
        return pltpu.make_async_remote_copy(
            source, bank.at[slot], send, recv, device_id={"segment": target}, device_id_type=MESH
        )

    def to_queue(source, slot, send, recv, target):
        return pltpu.make_async_remote_copy(
            source, queue.at[slot], send, recv, device_id={"segment": target}, device_id_type=MESH
        )

    def hand(n):
        return to_bank(
            out_v.at[n],
            n + images,
            hand_send.at[n],
            hand_recv.at[n + images],
            jnp.minimum(s + 1, SECTIONS - 1),
        )

    def arrived(recv):
        to_bank(out_v.at[0], spare, hand_send.at[0], recv, jnp.int32(0)).wait_recv()

    def to_five(source, n, send):
        @pl.when(n < 2 * images)
        def _():
            to_bank(source, side + 3 * images + n, send, mir_recv.at[n], jnp.int32(5)).start()

        @pl.when(n >= 2 * images)
        def _():
            to_queue(source, n - 2 * images, send, mir_recv.at[n], jnp.int32(5)).start()

    def wait_x(p):
        @pl.when((s == 0) & (p == images // PAIR))
        def _():
            load_fresh.wait()

        for k in range(PAIR):
            n = p * PAIR + k

            @pl.when((s > 0) & (n >= images))
            def _():
                arrived(hand_recv.at[n])

            @pl.when((s == 2) & (n >= images))
            def _():
                m = n - images
                to_queue(bank.at[n], m, rel_send.at[m], mir_recv.at[m], jnp.int32(6)).start()

    def convolve(slot, kind):
        g = jnp.where(kind == 0, gain[0:1], gain[1:2])
        b = jnp.where(kind == 0, shift[0:1], shift[1:2])
        fill_patches(bank[pl.ds(slot, PAIR)], g, b, patches)
        return jnp.dot(patches[...], w[kind], preferred_element_type=jnp.float32).reshape(PAIR, cells, channels)

    def step(p, start):
        early = encoder | ((s == half) & (p * PAIR >= images))
        if not start:
            pl.when(early)(lambda: wait_x(p))

        @pl.when((s == half + 1) & (p * PAIR >= 3 * images))
        def _():
            for k in range(PAIR):
                arrived(mir_recv.at[p * PAIR + k - 3 * images])

        if start:
            load_gain.wait()
            load_shift.wait()
            load_x.wait()
            for here, count in own_skips:
                pl.when(here)(load_q(count).wait)
            pl.when(encoder)(load_w[0].wait)
            pl.when(jnp.logical_not(encoder))(load_w[1].wait)
        n = p * PAIR
        kind = jnp.where(encoder, 0, 1)
        first = convolve(jnp.where(early, n, side + n), kind)
        bank[pl.ds(spare, PAIR)] = first
        if start:
            pl.when(encoder)(load_w[1].wait)
            pl.when(jnp.logical_not(encoder))(load_w[0].wait)
        else:
            pl.when(jnp.logical_not(early))(lambda: wait_x(p))
        second = convolve(jnp.where(encoder, spare, n), 1 - kind)
        total = bank[pl.ds(n, PAIR)] + second
        out_v[pl.ds(n, PAIR)] = jnp.where(encoder, total, total + bank[pl.ds(spare, PAIR)])
        if start:
            pl.semaphore_wait(barrier, SECTIONS - 1)
        for k in range(PAIR):
            send(p * PAIR + k)
        if not start:
            for k in range(PAIR):
                relay((p - 1) * PAIR + k)

    def send(n):
        @pl.when((s < SECTIONS - 1) & (n < handed))
        def _():
            hand(n).start()

        @pl.when(s == 0)
        def _():
            to_queue(out_v.at[n], n + 2 * images, mir_send.at[n], mir_recv.at[n], jnp.int32(7)).start()

        @pl.when((s == 1) & (n >= handed))
        def _():
            to_queue(out_v.at[n], n, mir_send.at[n], mir_recv.at[n], jnp.int32(6)).start()

        @pl.when((s == 2) & (n >= PAIR) & (n < handed))
        def _():
            to_bank(out_v.at[n], side + n, mir_send.at[n], mir_recv.at[n], jnp.int32(1)).start()

        @pl.when((s == 2) & ((n < PAIR) | (n >= handed)))
        def _():
            to_five(out_v.at[n], n, mir_send.at[n])

        @pl.when((s == 3) & (n >= handed))
        def _():
            to_queue(out_v.at[n], n - handed, mir_send.at[n], mir_recv.at[n], jnp.int32(4)).start()

        pltpu.make_async_copy(out_v.at[n], act.at[n], out_sem.at[n]).start()

    def relay(m):
        @pl.when((s == 1) & (m >= PAIR) & (m < handed))
        def _():
            arrived(mir_recv.at[m])
            to_five(bank.at[side + m], m, rel_send.at[m])

    step(jnp.int32(0), True)
    lax.fori_loop(1, pairs, lambda p, carry: (step(p, False), carry)[1], 0)

    def drain(n, carry):
        @pl.when((s < SECTIONS - 1) & (n < handed))
        def _():
            hand(n).wait_send()

        @pl.when((s == 0) | (s == 2) | (((s == 1) | (s == 3)) & (n >= handed)))
        def _():
            to_bank(out_v.at[n], spare, mir_send.at[n], mir_recv.at[n], jnp.int32(7)).wait_send()

        @pl.when((((s == 1) & (n >= PAIR)) | (s == 2)) & (n < handed))
        def _():
            to_bank(out_v.at[n], spare, rel_send.at[n], mir_recv.at[n], jnp.int32(6)).wait_send()

        @pl.when(((s == 4) & (n >= handed)) | ((s == 5) & (n >= 2 * images)) | (s >= 6))
        def _():
            arrived(mir_recv.at[n])

        pltpu.make_async_copy(out_v.at[n], act.at[n], out_sem.at[n]).wait()
        return carry

    lax.fori_loop(0, steps, drain, 0)
    pl.when(s == SECTIONS - 1)(keep_q.wait)


def place(act, queue, act_out, queue_out, zeros, sem):
    s = lax.axis_index("segment")
    depth = jnp.where(s < SECTIONS // 2, 0, 2 * s - SECTIONS + 1)
    images = zeros.shape[0]
    slots = queue.shape[0] // images
    ticks = act.shape[0] // images
    for t in range(ticks):
        rows = pl.ds(t * images, images)
        pltpu.make_async_copy(act.at[rows], act_out.at[rows], sem.at[t]).start()
    for k in range(slots):
        rows = pl.ds(k * images, images)
        pl.when(k < depth)(pltpu.make_async_copy(queue.at[rows], queue_out.at[rows], sem.at[ticks + k]).start)
    zeros[...] = jnp.zeros_like(zeros)
    for k in range(slots):
        rows = pl.ds(k * images, images)
        pl.when(k >= depth)(pltpu.make_async_copy(zeros, queue_out.at[rows], sem.at[ticks + k]).start)
    for t in range(ticks):
        rows = pl.ds(t * images, images)
        pltpu.make_async_copy(act.at[rows], act_out.at[rows], sem.at[t]).wait()
    for k in range(slots):
        rows = pl.ds(k * images, images)
        pltpu.make_async_copy(zeros, queue_out.at[rows], sem.at[ticks + k]).wait()


def per_device(handoff, fresh, skip_queue, conv_weight, norm_gain, norm_shift):
    _, images, height, width, channels = handoff.shape
    ticks = fresh.shape[0] + 1
    depth = skip_queue.shape[1]
    steps = images * ticks
    cells = height * width
    f32 = jnp.float32
    anywhere = pl.BlockSpec(memory_space=pl.ANY)
    shapes = (
        jax.ShapeDtypeStruct((steps, cells, channels), f32),
        jax.ShapeDtypeStruct((images * depth, cells, channels), f32),
    )
    operands = (
        handoff.reshape(images, cells, channels),
        fresh.reshape(steps - images, cells, channels),
        skip_queue.reshape(images * depth, cells, channels),
        conv_weight[0],
        norm_gain[0],
        norm_shift[0],
    )
    made = pl.pallas_call(
        functools.partial(window, images, ticks),
        out_shape=shapes,
        in_specs=[anywhere] * 6,
        out_specs=(anywhere, anywhere),
        scratch_shapes=[
            pltpu.VMEM((2, 9 * channels, channels), jnp.bfloat16),
            pltpu.VMEM((2, channels), f32),
            pltpu.VMEM((2, channels), f32),
            pltpu.VMEM((2 * steps + PAIR, cells, channels), f32),
            pltpu.VMEM((steps, cells, channels), f32),
            pltpu.VMEM((PAIR * cells, 9 * channels), jnp.bfloat16),
            pltpu.SemaphoreType.DMA((8,)),
            pltpu.SemaphoreType.DMA((steps,)),
            pltpu.SemaphoreType.DMA((steps,)),
            pltpu.SemaphoreType.DMA((steps,)),
            pltpu.SemaphoreType.DMA((steps,)),
            pltpu.SemaphoreType.DMA((steps,)),
            pltpu.SemaphoreType.DMA((steps,)),
        ],
        compiler_params=pltpu.CompilerParams(
            collective_id=0, has_side_effects=True, vmem_limit_bytes=36 << 20
        ),
        cost_estimate=pl.CostEstimate(
            flops=4 * steps * cells * 9 * channels * channels, bytes_accessed=20 << 20, transcendentals=0
        ),
        name="window",
    )(*[pltpu.with_memory_space_constraint(operand, pltpu.HBM) for operand in operands])
    act, queue = pl.pallas_call(
        place,
        out_shape=shapes,
        in_specs=[anywhere] * 2,
        out_specs=(anywhere, anywhere),
        scratch_shapes=[
            pltpu.VMEM((images, cells, channels), f32),
            pltpu.SemaphoreType.DMA((ticks + depth,)),
        ],
        compiler_params=pltpu.CompilerParams(vmem_limit_bytes=4 << 20),
        name="place",
    )(*made)
    return (
        act.reshape(1, ticks, images, height, width, channels),
        queue.reshape(1, depth, images, height, width, channels),
    )


def solution(mesh):
    return jax.shard_map(
        per_device,
        mesh=mesh,
        in_specs=(
            P("segment", "dp", None, None, None),
            P(None, "dp", None, None, None),
            P("segment", None, "dp", None, None, None),
            P("segment", None, None, None),
            P("segment", None, None),
            P("segment", None, None),
        ),
        out_specs=(
            P("segment", None, "dp", None, None, None),
            P("segment", None, "dp", None, None, None),
        ),
        check_vma=False,
    )
```

time: 294 us -> 74.2 us (0.25)
  waiting for transfers between devices: 178 us -> 0 us
  Pallas kernels: 0 us -> 73.5 us
  matrix products: 50.4 us -> 0 us
  starting transfers between devices: 27.7 us -> 0 us
  other arithmetic: 18.6 us -> 0 us
  local copies, waits for them, and re-layouts: 16.2 us -> 0 us
    ppermute x19 -> x0, waiting for transfers between devices: 178 us -> none  [the longest x15 130 us: from_partner(): return lax.ppermute(value, axis, pairs)]
    pallas_call x0 -> x2, Pallas kernels: none -> 73.5 us  [the longest x1 70.8 us: per_device(): pl.pallas_call(functools.partial(window, images, ticks), out_shape=shapes...]
    dot_general x10 -> x0, matrix products: 50.4 us -> none  [convolve(): jnp.dot(patches.reshape(images * height_cells * width_cells, 9 * channels...]
    ppermute x19 -> x0, starting transfers between devices: 27.7 us -> none  [the longest x15 16.4 us: from_partner(): return lax.ppermute(value, axis, pairs)]
    reduce_sum x35 -> x0, other arithmetic: 8.25 us -> none  [the longest x15 4.43 us: group_silu(): average = jnp.mean(grouped, axis=(1, 3), keepdims=True)]
    unnamed x94 -> x0, local copies, waits for them, and re-layouts: 6.33 us -> none
    slice x11 -> x0, local copies, waits for them, and re-layouts: 3.87 us -> none  [the longest x9 2.33 us: per_device(): pending[1:]]
    convert_element_type x10 -> x0, other arithmetic: 3.85 us -> none  [group_silu(): return jax.nn.silu(scaled).astype(jnp.bfloat16)]
  transfers between devices with their start and end apart: 19 -> 0, of which waited for: 19 -> 0; matrix products, arithmetic and copies ran while one was open for 4% -> 0% of each run, Pallas kernels for 0% -> 0%
where the time goes in v2:
time: 74.2 us
  Pallas kernels  73.5 us (99%)
    pallas_call x1, Pallas kernels, per_device(): pl.pallas_call(functools.partial(window, images, ticks), out_shape=shapes...  70.8 us
    pallas_call x1, Pallas kernels, per_device(): pl.pallas_call(place, out_shape=shapes, in_specs=[anywhere] * 2, out_spec...  2.75 us

profile of v2, /device:TPU:174, one launch (start us, length us, event | category | flops | bytes accessed | tf_op | source)
XLA Modules:
  0.0 74.2 jit_solution(3135961599627534753)
XLA Ops:
  0.6 70.8 %window.1 = (f32[20,64,512]{2,1,0:T(8,128)S(1)}, f32[28,64,512]{2,1,0:T(8,128)S(1)}) custom-call(f32[4,64,512]{2,1,0:T(8,128)} %bitcast.13, f32[16,64,512]{2,1,0:T(8,128)} %bitcast.12, f32[28,64,512]{2,1,0:T(8,128)} %bitcast.9, bf16[2,4608,512]{2,1,0:T(8,128)(2,1)} %bitcast.8, f32[2,512]{1,0:T(2,128)} %bitcast.14, f32[2,512]{1,0:T(2,128)} %bitcast.15), custom_call_target="tpu_custom_call" | custom-call | flops 12079595520 | bytes 20971520 | tf_op jit(solution)/shard_map/window/pallas_call | solution.py:342
  71.4 2.8 %place.1 = (f32[20,64,512]{2,1,0:T(8,128)}, f32[28,64,512]{2,1,0:T(8,128)}) custom-call(f32[20,64,512]{2,1,0:T(8,128)S(1)} %get-tuple-element.6.act, f32[28,64,512]{2,1,0:T(8,128)S(1)} %get-tuple-element.7.queue), custom_call_target="tpu_custom_call" | custom-call | tf_op jit(solution)/shard_map/place/pallas_call | solution.py:370

commit v3 on v2

--- a/solution.py
+++ b/solution.py
@@ -13,6 +13,11 @@
 LANES = 128
 PAIR = 2
 SECTIONS = 8
+PARTS = 1
+AHEAD = 0
+DIRECT = 2
+BY_ZERO = 14
+LATE = 1
 
 
 def merge_four(mean, spread, step):
@@ -143,36 +148,50 @@
     for k in range(1, SECTIONS):
         pl.semaphore_signal(barrier, 1, device_id={"segment": lax.rem(s + k, SECTIONS)}, device_id_type=MESH)
 
-    def to_bank(source, slot, send, recv, target):
+    def piece(h):
+        return pl.ds(h * (cells // PARTS), cells // PARTS)
+
+    def to_bank(source, slot, send, recv, target, h):
         return pltpu.make_async_remote_copy(
-            source, bank.at[slot], send, recv, device_id={"segment": target}, device_id_type=MESH
+            source.at[piece(h)],
+            bank.at[slot, piece(h)],
+            send,
+            recv,
+            device_id={"segment": target},
+            device_id_type=MESH,
         )
 
-    def to_queue(source, slot, send, recv, target):
+    def to_queue(source, slot, send, recv, target, h):
         return pltpu.make_async_remote_copy(
-            source, queue.at[slot], send, recv, device_id={"segment": target}, device_id_type=MESH
+            source.at[piece(h)],
+            queue.at[slot, piece(h)],
+            send,
+            recv,
+            device_id={"segment": target},
+            device_id_type=MESH,
         )
 
-    def hand(n):
+    def hand(n, h):
         return to_bank(
             out_v.at[n],
             n + images,
-            hand_send.at[n],
-            hand_recv.at[n + images],
+            hand_send.at[n, h],
+            hand_recv.at[n + images, h],
             jnp.minimum(s + 1, SECTIONS - 1),
+            h,
         )
 
     def arrived(recv):
-        to_bank(out_v.at[0], spare, hand_send.at[0], recv, jnp.int32(0)).wait_recv()
-
-    def to_five(source, n, send):
+        to_bank(out_v.at[0], spare, hand_send.at[0, 0], recv, jnp.int32(0), 0).wait_recv()
+
+    def to_five(source, n, send, h):
         @pl.when(n < 2 * images)
         def _():
-            to_bank(source, side + 3 * images + n, send, mir_recv.at[n], jnp.int32(5)).start()
+            to_bank(source, side + 3 * images + n, send, mir_recv.at[n, h], jnp.int32(5), h).start()
 
         @pl.when(n >= 2 * images)
         def _():
-            to_queue(source, n - 2 * images, send, mir_recv.at[n], jnp.int32(5)).start()
+            to_queue(source, n - 2 * images, send, mir_recv.at[n, h], jnp.int32(5), h).start()
 
     def wait_x(p):
         @pl.when((s == 0) & (p == images // PAIR))
@@ -181,15 +200,16 @@
 
         for k in range(PAIR):
             n = p * PAIR + k
-
-            @pl.when((s > 0) & (n >= images))
-            def _():
-                arrived(hand_recv.at[n])
-
-            @pl.when((s == 2) & (n >= images))
-            def _():
-                m = n - images
-                to_queue(bank.at[n], m, rel_send.at[m], mir_recv.at[m], jnp.int32(6)).start()
+            for h in range(PARTS):
+
+                @pl.when((s > 0) & (n >= images))
+                def _():
+                    arrived(hand_recv.at[n, h])
+
+                @pl.when((s == 2) & (n >= images + AHEAD))
+                def _():
+                    m = n - images
+                    to_queue(bank.at[n], m, rel_send.at[m, h], mir_recv.at[m, h], jnp.int32(6), h).start()
 
     def convolve(slot, kind):
         g = jnp.where(kind == 0, gain[0:1], gain[1:2])
@@ -205,7 +225,8 @@
         @pl.when((s == half + 1) & (p * PAIR >= 3 * images))
         def _():
             for k in range(PAIR):
-                arrived(mir_recv.at[p * PAIR + k - 3 * images])
+                for h in range(PARTS):
+                    arrived(mir_recv.at[p * PAIR + k - 3 * images, h])
 
         if start:
             load_gain.wait()
@@ -236,57 +257,80 @@
                 relay((p - 1) * PAIR + k)
 
     def send(n):
-        @pl.when((s < SECTIONS - 1) & (n < handed))
-        def _():
-            hand(n).start()
-
-        @pl.when(s == 0)
-        def _():
-            to_queue(out_v.at[n], n + 2 * images, mir_send.at[n], mir_recv.at[n], jnp.int32(7)).start()
-
-        @pl.when((s == 1) & (n >= handed))
-        def _():
-            to_queue(out_v.at[n], n, mir_send.at[n], mir_recv.at[n], jnp.int32(6)).start()
-
-        @pl.when((s == 2) & (n >= PAIR) & (n < handed))
-        def _():
-            to_bank(out_v.at[n], side + n, mir_send.at[n], mir_recv.at[n], jnp.int32(1)).start()
-
-        @pl.when((s == 2) & ((n < PAIR) | (n >= handed)))
-        def _():
-            to_five(out_v.at[n], n, mir_send.at[n])
-
-        @pl.when((s == 3) & (n >= handed))
-        def _():
-            to_queue(out_v.at[n], n - handed, mir_send.at[n], mir_recv.at[n], jnp.int32(4)).start()
+        for h in range(PARTS):
+            pl.when((s < SECTIONS - 1) & (n < handed))(lambda h=h: hand(n, h).start())
+
+        for h in range(PARTS):
+
+            @pl.when(s == 0)
+            def _():
+                to_queue(
+                    out_v.at[n], n + 2 * images, mir_send.at[n, h], mir_recv.at[n, h], jnp.int32(7), h
+                ).start()
+
+            @pl.when((s == 1) & ((n < AHEAD) | (n >= handed)))
+            def _():
+                to_queue(out_v.at[n], n, mir_send.at[n, h], mir_recv.at[n, h], jnp.int32(6), h).start()
+
+            @pl.when((s == 2) & (n >= DIRECT) & (n < handed + LATE))
+            def _():
+                to_bank(out_v.at[n], side + n, mir_send.at[n, h], mir_recv.at[n, h], jnp.int32(1), h).start()
+
+            @pl.when((s == 2) & ((n < DIRECT) | (n >= handed + LATE)))
+            def _():
+                to_five(out_v.at[n], n, mir_send.at[n, h], h)
+
+            @pl.when((s == 3) & (n >= handed))
+            def _():
+                to_queue(out_v.at[n], n - handed, mir_send.at[n, h], mir_recv.at[n, h], jnp.int32(4), h).start()
 
         pltpu.make_async_copy(out_v.at[n], act.at[n], out_sem.at[n]).start()
 
     def relay(m):
-        @pl.when((s == 1) & (m >= PAIR) & (m < handed))
-        def _():
-            arrived(mir_recv.at[m])
-            to_five(bank.at[side + m], m, rel_send.at[m])
+        for h in range(PARTS):
+
+            @pl.when((s == 1) & (m >= DIRECT) & (m < handed + LATE))
+            def _():
+                arrived(mir_recv.at[m, h])
+
+                @pl.when(m == BY_ZERO)
+                def _():
+                    to_bank(
+                        bank.at[side + m], side + m, rel_send.at[m, h], mir_recv.at[m, h], jnp.int32(0), h
+                    ).start()
+
+                @pl.when(m != BY_ZERO)
+                def _():
+                    to_five(bank.at[side + m], m, rel_send.at[m, h], h)
 
     step(jnp.int32(0), True)
     lax.fori_loop(1, pairs, lambda p, carry: (step(p, False), carry)[1], 0)
 
+    @pl.when(s == 0)
+    def _():
+        for h in range(PARTS):
+            arrived(mir_recv.at[BY_ZERO, h])
+            to_five(bank.at[side + BY_ZERO], jnp.int32(BY_ZERO), rel_send.at[BY_ZERO, h], h)
+
     def drain(n, carry):
-        @pl.when((s < SECTIONS - 1) & (n < handed))
-        def _():
-            hand(n).wait_send()
-
-        @pl.when((s == 0) | (s == 2) | (((s == 1) | (s == 3)) & (n >= handed)))
-        def _():
-            to_bank(out_v.at[n], spare, mir_send.at[n], mir_recv.at[n], jnp.int32(7)).wait_send()
-
-        @pl.when((((s == 1) & (n >= PAIR)) | (s == 2)) & (n < handed))
-        def _():
-            to_bank(out_v.at[n], spare, rel_send.at[n], mir_recv.at[n], jnp.int32(6)).wait_send()
-
-        @pl.when(((s == 4) & (n >= handed)) | ((s == 5) & (n >= 2 * images)) | (s >= 6))
-        def _():
-            arrived(mir_recv.at[n])
+        for h in range(PARTS):
+            pl.when((s < SECTIONS - 1) & (n < handed))(lambda h=h: hand(n, h).wait_send())
+
+            @pl.when((s == 0) | (s == 2) | ((s == 1) & (n < AHEAD)) | (((s == 1) | (s == 3)) & (n >= handed)))
+            def _():
+                to_bank(out_v.at[n], spare, mir_send.at[n, h], mir_recv.at[n, h], jnp.int32(7), h).wait_send()
+
+            @pl.when(
+                ((s == 0) & (n == BY_ZERO))
+                | ((s == 1) & (n >= DIRECT) & (n < handed + LATE))
+                | ((s == 2) & (n >= AHEAD) & (n < handed))
+            )
+            def _():
+                to_bank(out_v.at[n], spare, rel_send.at[n, h], mir_recv.at[n, h], jnp.int32(6), h).wait_send()
+
+            @pl.when(((s == 4) & (n >= handed)) | ((s == 5) & (n >= 2 * images)) | (s >= 6))
+            def _():
+                arrived(mir_recv.at[n, h])
 
         pltpu.make_async_copy(out_v.at[n], act.at[n], out_sem.at[n]).wait()
         return carry
@@ -352,11 +396,11 @@
             pltpu.VMEM((steps, cells, channels), f32),
             pltpu.VMEM((PAIR * cells, 9 * channels), jnp.bfloat16),
             pltpu.SemaphoreType.DMA((8,)),
-            pltpu.SemaphoreType.DMA((steps,)),
-            pltpu.SemaphoreType.DMA((steps,)),
-            pltpu.SemaphoreType.DMA((steps,)),
-            pltpu.SemaphoreType.DMA((steps,)),
-            pltpu.SemaphoreType.DMA((steps,)),
+            pltpu.SemaphoreType.DMA((steps, PARTS)),
+            pltpu.SemaphoreType.DMA((steps, PARTS)),
+            pltpu.SemaphoreType.DMA((steps, PARTS)),
+            pltpu.SemaphoreType.DMA((steps, PARTS)),
+            pltpu.SemaphoreType.DMA((steps, PARTS)),
             pltpu.SemaphoreType.DMA((steps,)),
         ],
         compiler_params=pltpu.CompilerParams(

time: 74.2 us -> 71.4 us (0.962)
  Pallas kernels: 73.5 us -> 70.7 us
    pallas_call x1, Pallas kernels: 70.8 us -> 68 us  [per_device(): pl.pallas_call(functools.partial(window, images, ticks), out_shape=shapes...]
where the time goes in v3:
time: 71.4 us; the launch traced here: 71.3 us
  Pallas kernels  70.7 us (99%)
    pallas_call x1, Pallas kernels, per_device(): pl.pallas_call(functools.partial(window, images, ticks), out_shape=shapes...  68 us
    pallas_call x1, Pallas kernels, per_device(): pl.pallas_call(place, out_shape=shapes, in_specs=[anywhere] * 2, out_spec...  2.75 us

profile of v3, /device:TPU:174, one launch (start us, length us, event | category | flops | bytes accessed | tf_op | source)
XLA Modules:
  0.0 71.3 jit_solution(7342375726937273175)
XLA Ops:
  0.6 68.0 %window.1 = (f32[20,64,512]{2,1,0:T(8,128)S(1)}, f32[28,64,512]{2,1,0:T(8,128)S(1)}) custom-call(f32[4,64,512]{2,1,0:T(8,128)} %bitcast.13, f32[16,64,512]{2,1,0:T(8,128)} %bitcast.12, f32[28,64,512]{2,1,0:T(8,128)} %bitcast.9, bf16[2,4608,512]{2,1,0:T(8,128)(2,1)} %bitcast.8, f32[2,512]{1,0:T(2,128)} %bitcast.14, f32[2,512]{1,0:T(2,128)} %bitcast.15), custom_call_target="tpu_custom_call" | custom-call | flops 12079595520 | bytes 20971520 | tf_op jit(solution)/shard_map/window/pallas_call | solution.py:386
  68.6 2.8 %place.1 = (f32[20,64,512]{2,1,0:T(8,128)}, f32[28,64,512]{2,1,0:T(8,128)}) custom-call(f32[20,64,512]{2,1,0:T(8,128)S(1)} %get-tuple-element.6.act, f32[28,64,512]{2,1,0:T(8,128)S(1)} %get-tuple-element.7.queue), custom_call_target="tpu_custom_call" | custom-call | tf_op jit(solution)/shard_map/place/pallas_call | solution.py:414

commit v4 on v3

--- a/solution.py
+++ b/solution.py
@@ -15,9 +15,10 @@
 SECTIONS = 8
 PARTS = 1
 AHEAD = 0
-DIRECT = 2
+DIRECT = 1
 BY_ZERO = 14
-LATE = 1
+CUT = 24
+HELD = 2
 
 
 def merge_four(mean, spread, step):
@@ -193,6 +194,16 @@
         def _():
             to_queue(source, n - 2 * images, send, mir_recv.at[n, h], jnp.int32(5), h).start()
 
+    def split_to_five(source, slot, send, rows):
+        return pltpu.make_async_remote_copy(
+            source.at[slot, rows],
+            queue.at[handed - 2 * images, rows],
+            send.at[handed, 0],
+            mir_recv.at[handed, 0],
+            device_id={"segment": jnp.int32(5)},
+            device_id_type=MESH,
+        )
+
     def wait_x(p):
         @pl.when((s == 0) & (p == images // PAIR))
         def _():
@@ -262,7 +273,7 @@
 
         for h in range(PARTS):
 
-            @pl.when(s == 0)
+            @pl.when((s == 0) & (n < steps - HELD))
             def _():
                 to_queue(
                     out_v.at[n], n + 2 * images, mir_send.at[n, h], mir_recv.at[n, h], jnp.int32(7), h
@@ -272,24 +283,36 @@
             def _():
                 to_queue(out_v.at[n], n, mir_send.at[n, h], mir_recv.at[n, h], jnp.int32(6), h).start()
 
-            @pl.when((s == 2) & (n >= DIRECT) & (n < handed + LATE))
+            @pl.when((s == 2) & (n >= DIRECT) & (n < handed))
             def _():
                 to_bank(out_v.at[n], side + n, mir_send.at[n, h], mir_recv.at[n, h], jnp.int32(1), h).start()
 
-            @pl.when((s == 2) & ((n < DIRECT) | (n >= handed + LATE)))
+            @pl.when((s == 2) & ((n < DIRECT) | (n > handed)))
             def _():
                 to_five(out_v.at[n], n, mir_send.at[n, h], h)
 
             @pl.when((s == 3) & (n >= handed))
             def _():
                 to_queue(out_v.at[n], n - handed, mir_send.at[n, h], mir_recv.at[n, h], jnp.int32(4), h).start()
+
+        @pl.when((s == 2) & (n == handed))
+        def _():
+            split_to_five(out_v, handed, mir_send, slice(0, CUT)).start()
+            pltpu.make_async_remote_copy(
+                out_v.at[handed, CUT:],
+                bank.at[side + handed, CUT:],
+                mir_send.at[handed, 0],
+                mir_recv.at[handed, 0],
+                device_id={"segment": jnp.int32(1)},
+                device_id_type=MESH,
+            ).start()
 
         pltpu.make_async_copy(out_v.at[n], act.at[n], out_sem.at[n]).start()
 
     def relay(m):
         for h in range(PARTS):
 
-            @pl.when((s == 1) & (m >= DIRECT) & (m < handed + LATE))
+            @pl.when((s == 1) & (m >= DIRECT) & (m < handed))
             def _():
                 arrived(mir_recv.at[m, h])
 
@@ -303,6 +326,12 @@
                 def _():
                     to_five(bank.at[side + m], m, rel_send.at[m, h], h)
 
+        @pl.when((s == 1) & (m == handed))
+        def _():
+            late = split_to_five(bank, side + handed, rel_send, slice(CUT, None))
+            late.wait_recv()
+            late.start()
+
     step(jnp.int32(0), True)
     lax.fori_loop(1, pairs, lambda p, carry: (step(p, False), carry)[1], 0)
 
@@ -311,6 +340,11 @@
         for h in range(PARTS):
             arrived(mir_recv.at[BY_ZERO, h])
             to_five(bank.at[side + BY_ZERO], jnp.int32(BY_ZERO), rel_send.at[BY_ZERO, h], h)
+        for n in range(steps - HELD, steps):
+            for h in range(PARTS):
+                to_queue(
+                    out_v.at[n], n + 2 * images, mir_send.at[n, h], mir_recv.at[n, h], jnp.int32(7), h
+                ).start()
 
     def drain(n, carry):
         for h in range(PARTS):
@@ -322,7 +356,7 @@
 
             @pl.when(
                 ((s == 0) & (n == BY_ZERO))
-                | ((s == 1) & (n >= DIRECT) & (n < handed + LATE))
+                | ((s == 1) & (n >= DIRECT) & (n < handed))
                 | ((s == 2) & (n >= AHEAD) & (n < handed))
             )
             def _():
@@ -336,6 +370,7 @@
         return carry
 
     lax.fori_loop(0, steps, drain, 0)
+    pl.when(s == 1)(split_to_five(bank, side + handed, rel_send, slice(CUT, None)).wait_send)
     pl.when(s == SECTIONS - 1)(keep_q.wait)
 
 

time: 71.4 us -> 71.1 us (level)
  no operation moved by 1% of the time
where the time goes in v4:
time: 71.1 us; the launch traced here: 71 us
  Pallas kernels  70.4 us (99%)
    pallas_call x1, Pallas kernels, per_device(): pl.pallas_call(functools.partial(window, images, ticks), out_shape=shapes...  67.6 us
    pallas_call x1, Pallas kernels, per_device(): pl.pallas_call(place, out_shape=shapes, in_specs=[anywhere] * 2, out_spec...  2.75 us

profile of v4, /device:TPU:174, one launch (start us, length us, event | category | flops | bytes accessed | tf_op | source)
XLA Modules:
  0.0 71.0 jit_solution(18211894714030092316)
XLA Ops:
  0.6 67.6 %window.1 = (f32[20,64,512]{2,1,0:T(8,128)S(1)}, f32[28,64,512]{2,1,0:T(8,128)S(1)}) custom-call(f32[4,64,512]{2,1,0:T(8,128)} %bitcast.13, f32[16,64,512]{2,1,0:T(8,128)} %bitcast.12, f32[28,64,512]{2,1,0:T(8,128)} %bitcast.9, bf16[2,4608,512]{2,1,0:T(8,128)(2,1)} %bitcast.8, f32[2,512]{1,0:T(2,128)} %bitcast.14, f32[2,512]{1,0:T(2,128)} %bitcast.15), custom_call_target="tpu_custom_call" | custom-call | flops 12079595520 | bytes 20971520 | tf_op jit(solution)/shard_map/window/pallas_call | solution.py:421
  68.3 2.8 %place.1 = (f32[20,64,512]{2,1,0:T(8,128)}, f32[28,64,512]{2,1,0:T(8,128)}) custom-call(f32[20,64,512]{2,1,0:T(8,128)S(1)} %get-tuple-element.6.act, f32[28,64,512]{2,1,0:T(8,128)S(1)} %get-tuple-element.7.queue), custom_call_target="tpu_custom_call" | custom-call | tf_op jit(solution)/shard_map/place/pallas_call | solution.py:449

commit v5 on v4

--- a/solution.py
+++ b/solution.py
@@ -263,9 +263,13 @@
             pl.semaphore_wait(barrier, SECTIONS - 1)
         for k in range(PAIR):
             send(p * PAIR + k)
+        keep(n).start()
         if not start:
             for k in range(PAIR):
                 relay((p - 1) * PAIR + k)
+
+    def keep(n):
+        return pltpu.make_async_copy(out_v.at[pl.ds(n, PAIR)], act.at[pl.ds(n, PAIR)], out_sem.at[n])
 
     def send(n):
         for h in range(PARTS):
@@ -307,7 +311,6 @@
                 device_id_type=MESH,
             ).start()
 
-        pltpu.make_async_copy(out_v.at[n], act.at[n], out_sem.at[n]).start()
 
     def relay(m):
         for h in range(PARTS):
@@ -366,7 +369,7 @@
             def _():
                 arrived(mir_recv.at[n, h])
 
-        pltpu.make_async_copy(out_v.at[n], act.at[n], out_sem.at[n]).wait()
+        pl.when(lax.rem(n, PAIR) == 0)(keep(n).wait)
         return carry
 
     lax.fori_loop(0, steps, drain, 0)

time: 71.1 us -> 71.1 us (level)
  no operation moved by 1% of the time
where the time goes in v5:
time: 71.1 us; the launch traced here: 71 us
  Pallas kernels  70.3 us (99%)
    pallas_call x1, Pallas kernels, per_device(): pl.pallas_call(functools.partial(window, images, ticks), out_shape=shapes...  67.6 us
    pallas_call x1, Pallas kernels, per_device(): pl.pallas_call(place, out_shape=shapes, in_specs=[anywhere] * 2, out_spec...  2.75 us

profile of v5, /device:TPU:174, one launch (start us, length us, event | category | flops | bytes accessed | tf_op | source)
XLA Modules:
  0.0 71.0 jit_solution(7460025511791461494)
XLA Ops:
  0.6 67.6 %window.1 = (f32[20,64,512]{2,1,0:T(8,128)S(1)}, f32[28,64,512]{2,1,0:T(8,128)S(1)}) custom-call(f32[4,64,512]{2,1,0:T(8,128)} %bitcast.13, f32[16,64,512]{2,1,0:T(8,128)} %bitcast.12, f32[28,64,512]{2,1,0:T(8,128)} %bitcast.9, bf16[2,4608,512]{2,1,0:T(8,128)(2,1)} %bitcast.8, f32[2,512]{1,0:T(2,128)} %bitcast.14, f32[2,512]{1,0:T(2,128)} %bitcast.15), custom_call_target="tpu_custom_call" | custom-call | flops 12079595520 | bytes 20971520 | tf_op jit(solution)/shard_map/window/pallas_call | solution.py:424
  68.2 2.8 %place.1 = (f32[20,64,512]{2,1,0:T(8,128)}, f32[28,64,512]{2,1,0:T(8,128)}) custom-call(f32[20,64,512]{2,1,0:T(8,128)S(1)} %get-tuple-element.6.act, f32[28,64,512]{2,1,0:T(8,128)S(1)} %get-tuple-element.7.queue), custom_call_target="tpu_custom_call" | custom-call | tf_op jit(solution)/shard_map/place/pallas_call | solution.py:452
